TPU v7x, 128 devices: a whole 4x4x4 slice. The times are simulated.
128 devices in a mesh: row: 16 (over y_hi, z, core), col: 8 (over x, y_lo).
Axes of the slice: x: 4, y: 4 (y_hi: 2, y_lo: 2; y = y_hi * 2 + y_lo), z: 4, core: 2. Of those that a mesh axis runs over, the one named last changes fastest.
Arguments:
- features: bfloat16 [65536, 128], P('col', 'row'), may hold values from -6 to 6
- weight: bfloat16 [128, 128], replicated, may hold values from -0.5 to 0.5
- tiles: bfloat16 [16, 8, 256, 128, 128], P('row', 'col'), may hold values from 0 to 0.019897461
- tile_rows: int32 [16, 8, 256], P('row', 'col'), may hold values from 0 to 31, as said below
- tile_cols: int32 [16, 8, 256], P('row', 'col'), may hold values from 0 to 63
- tile_count: int32 [16, 8], P('row', 'col'), may hold values from 1 to 256, as said below
- cotangent: bfloat16 [65536, 128], P(('row', 'col')), may hold values from -6 to 6
Outputs:
- activated: bfloat16 [65536, 128], P(('row', 'col'))
- grad_weight: float32 [128, 128], P('row')
- grad_features: bfloat16 [65536, 128], P('col', 'row')
Inputs may be any that keep to these rules, and one draw needn't show every extreme that they name: Within one grid cell the live and padded slots name distinct (tile_rows, tile_cols) pairs. `tile_count`: some grid cell is full in every draw.
All inputs are finite; a program needn't handle non-finite values.
Results may differ from a plain program's by a relative error of at most 0.006.
Values may be sent and summed in bfloat16 or wider, within the bound.
A program may use at most 128 MiB of HBM per device.

v0:
```python
import jax
import jax.numpy as jnp
from jax import lax
from jax.sharding import PartitionSpec as P

F = 128
BLK = 128
BR = 32
TILE_CAP = 256


def on_device(features, weight, tiles, tile_rows, tile_cols, tile_count, cotangent):
    panel_rows = features.shape[0]
    narrow = features.shape[1]
    ncols = panel_rows // BLK
    tile_set = tiles[0, 0]
    local_rows = tile_rows[0, 0]
    local_cols = tile_cols[0, 0]
    count = tile_count[0, 0]
    slots = jnp.arange(TILE_CAP, dtype=jnp.int32)
    live = slots < count
    weight_part = lax.dynamic_slice_in_dim(weight, lax.axis_index("row") * narrow, narrow, 0)
    partial_panel = jnp.dot(features, weight_part, preferred_element_type=jnp.float32)
    summed = lax.psum(partial_panel, "row")
    hidden = summed.astype(jnp.bfloat16)
    picked = hidden.reshape(ncols, BLK, F)[local_cols]
    prods = jnp.einsum("tij,tjf->tif", tile_set, picked, preferred_element_type=jnp.float32)
    prods = jnp.where(live[:, None, None], prods, jnp.zeros_like(prods))
    partial_rows = (
        jnp.zeros((BR, BLK, F), jnp.float32).at[local_rows].add(prods).reshape(BR * BLK, F)
    )
    pre = lax.psum_scatter(partial_rows, "col", scatter_dimension=0, tiled=True)
    sig = jax.nn.sigmoid(pre)
    activated = (pre * sig).astype(jnp.bfloat16)
    grad_pre = (cotangent.astype(jnp.float32) * sig * (1.0 + pre * (1.0 - sig))).astype(
        jnp.bfloat16
    )
    grad_rows = lax.all_gather(grad_pre, "col", axis=0, tiled=True)
    picked_back = grad_rows.reshape(BR, BLK, F)[local_rows]
    back_prods = jnp.einsum(
        "tji,tjf->tif", tile_set, picked_back, preferred_element_type=jnp.float32
    )
    back_prods = jnp.where(live[:, None, None], back_prods, jnp.zeros_like(back_prods))
    partial_cols = (
        jnp.zeros((ncols, BLK, F), jnp.float32)
        .at[local_cols]
        .add(back_prods)
        .reshape(panel_rows, F)
    )
    grad_hidden = lax.psum(partial_cols, "row").astype(jnp.bfloat16)
    weight_term = lax.dot_general(
        features, grad_hidden, (((0,), (0,)), ((), ())), preferred_element_type=jnp.float32
    )
    grad_weight = lax.psum(weight_term, "col")
    grad_features = lax.dot_general(
        grad_hidden, weight_part, (((1,), (1,)), ((), ())), preferred_element_type=jnp.float32
    ).astype(jnp.bfloat16)
    return (activated, grad_weight, grad_features)


def solution(mesh):
    return jax.shard_map(
        on_device,
        mesh=mesh,
        in_specs=(
            P("col", "row"),
            P(),
            P("row", "col", None, None, None),
            P("row", "col", None),
            P("row", "col", None),
            P("row", "col"),
            P(("row", "col"), None),
        ),
        out_specs=(P(("row", "col"), None), P("row", None), P("col", "row")),
        check_vma=False,
    )
```

profile of v0, /device:TPU:0, one launch (start us, length us, event | category | flops | bytes accessed | tf_op | source)
XLA Modules:
  0.0 475.5 jit_solution(12710308483521831545)
XLA Ops:
  7.2 0.0 reduce-scatter.2.cloned.1.call-start
  7.2 0.8 copy-done
  8.1 3.4 convolution_bitcast_fusion
  11.4 88.5 %all-reduce.2 = bf16[8192,128]{0,1:T(8,128)(2,1)} all-reduce(f32[8192,128]{0,1:T(8,128)} %convolution_bitcast_fusion), channel_id=1, replica_groups=mesh['row'=16,'col'=8] {'row'}, use_global_device_ids=true, to_apply=%region_0.0 | all-reduce | flops 1048576 | bytes 6291456 | tf_op jit(solution)/shard_map/psum | solution.py:24
  99.9 3.2 copy.19
  103.8 8.6 %gather_fusion = bf16[256,128,128]{2,1,0:T(8,128)(2,1)} fusion(bf16[64,128,128]{2,1,0:T(8,128)(2,1)S(1)} %bitcast.34, s32[1024]{0:T(1024)S(1)} %pad_clamp_fusion.1), kind=kCustom, calls=%fused_computation | custom fusion | bytes 16778240 | tf_op jit(solution)/shard_map/gather | solution.py:26
  112.5 13.1 %select_bitcast_fusion.1 = f32[256,128,128]{1,2,0:T(8,128)} fusion(bf16[256,128,128]{2,1,0:T(8,128)(2,1)} %gather_fusion, bf16[1,1,256,128,128]{4,3,2,1,0:T(8,128)(2,1)} %param.9, pred[256]{0:T(512)(128)(4,1)S(1)} %iota_compare_fusion), kind=kOutput, calls=%fused_computation.5 | convolution fusion | flops 1077936128 | bytes 33554688 | tf_op jit(solution)/shard_map/tij,tjf->tif/dot_general | solution.py:27
  125.6 17.5 %copy.14 = f32[256,128,128]{2,1,0:T(8,128)} copy(f32[256,128,128]{1,2,0:T(8,128)} %select_bitcast_fusion.1) | data formatting | bytes 33554432 | tf_op jit(solution)/shard_map/jit(_where)/select_n | solution.py:28
  143.1 0.2 broadcast_in_dim.23
  143.3 33.2 %scatter_fusion = f32[32,128,128]{2,1,0:T(8,128)S(1)} fusion(f32[32,128,128]{2,1,0:T(8,128)S(1)} %broadcast_in_dim.23, s32[256]{0:T(256)S(1)} %bitcast.37, f32[256,128,128]{2,1,0:T(8,128)} %copy.14), kind=kCustom, calls=%fused_computation.2 | custom fusion | flops 4194304 | bytes 50332672 | tf_op jit(solution)/shard_map/scatter-add | solution.py:30
  176.5 1.3 copy-done.1
  177.9 0.2 all-gather.2.cloned.1.call-start
  178.1 47.9 %reduce-scatter.2.cloned.1.call-done = f32[512,128]{1,0:T(8,128)} async-done(((f32[4096,128]{1,0:T(8,128)}), f32[512,128]{1,0:T(8,128)}) %reduce-scatter.2.cloned.1.call-update) | async-done | bytes 262160 | tf_op jit(solution)/shard_map/reduce_scatter | solution.py:32
  226.0 1.8 multiply_convert_fusion
  227.8 40.4 %all-gather.2.cloned.1.call-done = bf16[4096,128]{1,0:T(8,128)(2,1)} async-done(((bf16[512,128]{1,0:T(8,128)(2,1)}), bf16[4096,128]{1,0:T(8,128)(2,1)}) %all-gather.2.cloned.1.call-update) | async-done | bytes 1048592 | tf_op jit(solution)/shard_map/all_gather | solution.py:38
  268.2 9.8 %gather_fusion.1 = bf16[256,128,128]{2,1,0:T(8,128)(2,1)} fusion(bf16[32,128,128]{2,1,0:T(8,128)(2,1)} %bitcast.33, s32[1024]{0:T(1024)S(1)} %pad_clamp_fusion), kind=kCustom, calls=%fused_computation.1 | custom fusion | bytes 16778240 | tf_op jit(solution)/shard_map/gather | solution.py:39
  278.1 15.4 %select_bitcast_fusion = f32[256,128,128]{1,2,0:T(8,128)} fusion(bf16[256,128,128]{2,1,0:T(8,128)(2,1)} %gather_fusion.1, bf16[1,1,256,128,128]{4,3,2,1,0:T(8,128)(2,1)} %param.9, pred[256]{0:T(512)(128)(4,1)S(1)} %iota_compare_fusion), kind=kOutput, calls=%fused_computation.4 | convolution fusion | flops 1077936128 | bytes 33554688 | tf_op jit(solution)/shard_map/tji,tjf->tif/dot_general | solution.py:40
  293.5 17.5 %copy.16 = f32[256,128,128]{2,1,0:T(8,128)} copy(f32[256,128,128]{1,2,0:T(8,128)} %select_bitcast_fusion) | data formatting | bytes 33554432 | tf_op jit(solution)/shard_map/jit(_where)/select_n | solution.py:43
  310.9 2.4 broadcast_in_dim.25
  313.4 51.5 %scatter_fusion.1 = f32[64,128,128]{2,1,0:T(8,128)} fusion(f32[64,128,128]{2,1,0:T(8,128)} %broadcast_in_dim.25, s32[256]{0:T(256)S(1)} %bitcast.36, f32[256,128,128]{2,1,0:T(8,128)} %copy.16), kind=kCustom, calls=%fused_computation.3 | custom fusion | flops 4194304 | bytes 50332672 | tf_op jit(solution)/shard_map/scatter-add | solution.py:47
  364.9 83.3 %all-reduce.3 = bf16[8192,128]{1,0:T(8,128)(2,1)S(1)} all-reduce(f32[8192,128]{1,0:T(8,128)} %bitcast.32), channel_id=1, replica_groups=mesh['row'=16,'col'=8] {'row'}, use_global_device_ids=true, to_apply=%region_4.5 | all-reduce | flops 1048576 | bytes 6291456 | tf_op jit(solution)/shard_map/psum | solution.py:50
  448.2 2.0 convolution_convert_fusion
  450.2 0.4 convolution_bitcast_fusion.1
  450.6 18.1 %psum.23 = f32[8,128]{1,0:T(8,128)} all-reduce(f32[8,128]{1,0:T(8,128)S(1)} %convolution_bitcast_fusion.1), channel_id=1, replica_groups=mesh['row'=16,'col'=8] {'col'}, use_global_device_ids=true, to_apply=%region_5.6 | all-reduce | flops 1024 | bytes 8192 | tf_op jit(solution)/shard_map/psum | solution.py:54
  (15 shorter events, 0.1 us)
Async XLA Ops:
  7.2 0.9 copy-start
  7.2 96.0 %copy-start.3 = (s32[1,1,256]{2,1,0:T(1,128)S(1)}, s32[1,1,256]{2,1,0:T(1,128)}, u32[]{:S(2)}) copy-start(s32[1,1,256]{2,1,0:T(1,128)} %param.11) | copy-start | bytes 3076
  7.2 218.8 %reduce-scatter.2.cloned.1.call-start = ((), (), s32[]{:S(2)}) async-start(), calls=%async_computation.1 | async-start | bytes 2359296 | tf_op jit(solution)/shard_map/reduce_scatter | solution.py:32
  125.6 17.5 %copy-start.4 = (s32[1,1,256]{2,1,0:T(1,128)S(1)}, s32[1,1,256]{2,1,0:T(1,128)}, u32[]{:S(2)}) copy-start(s32[1,1,256]{2,1,0:T(1,128)} %param.10) | copy-start | bytes 3076
  143.3 82.7 %copy-start.2 = (bf16[512,128]{1,0:T(8,128)(2,1)S(1)}, bf16[512,128]{1,0:T(8,128)(2,1)}, u32[]{:S(2)}) copy-start(bf16[512,128]{1,0:T(8,128)(2,1)} %param.13) | copy-start | bytes 393220
  176.5 1.4 copy-start.1
  177.9 90.3 %all-gather.2.cloned.1.call-start = ((), (), s32[]{:S(2)}) async-start(), calls=%async_computation.2 | async-start | bytes 1179648 | tf_op jit(solution)/shard_map/all_gather | solution.py:38
Sparse Core Ops, SparseCore 0:
  178.0 47.9 reduce-scatter.1
  228.2 39.9 all-gather.1
where the time goes:
time: 477 us; the launch traced here: 476 us
  blocking collectives  190 us (40%)
  waiting for transfers between devices  88.3 us (19%)
  other arithmetic  86.5 us (18%)
  local copies, waits for them, and re-layouts  61.5 us (13%)
  matrix products  34.3 us (7%)
  between operations  14.8 us (3%)
    psum x1, blocking collectives, on_device(): summed = lax.psum(partial_panel, 'row')  88.5 us
    psum x1, blocking collectives, on_device(): grad_hidden = lax.psum(partial_cols, 'row').astype(jnp.bfloat16)  83.3 us
    scatter-add x1, other arithmetic, on_device(): partial_cols = jnp.zeros((ncols, BLK, F), jnp.float32).at[local_cols].add...  51.5 us
    reduce_scatter x1, waiting for transfers between devices, on_device(): pre = lax.psum_scatter(partial_rows, 'col', scatter_dimension=0, tiled=True)  47.9 us
    all_gather x1, waiting for transfers between devices, on_device(): grad_rows = lax.all_gather(grad_pre, 'col', axis=0, tiled=True)  40.4 us
    scatter-add x1, other arithmetic, on_device(): jnp.zeros((BR, BLK, F), jnp.float32).at[local_rows].add(prods)  33.2 us
    psum x1, blocking collectives, on_device(): grad_weight = lax.psum(weight_term, 'col')  18.1 us
    select_n x1, local copies, waits for them, and re-layouts, on_device(): prods = jnp.where(live[:, None, None], prods, jnp.zeros_like(prods))  17.5 us
  transfers between devices with their start and end apart: 2, of which 2 were waited for; matrix products, arithmetic and copies ran while one was open for 0% of the time, Pallas kernels for 0%

commit v1 on v0

v1 whole, which is shorter than its diff:
```python
import functools

import jax
import jax.numpy as jnp
from jax import lax
from jax.experimental import pallas as pl
from jax.experimental.pallas import tpu as pltpu
from jax.sharding import PartitionSpec as P

F = 128
BLK = 128
NROW = 16
NCOL = 8
BR = 32
BC = 64
TILE_CAP = 256
CHUNK = 512
SUB = CHUNK // BLK
PER = F // NROW
STEP = 16
MIB = 1024 * 1024
MESH = pl.DeviceIdType.MESH
CHIPS = [(0, 1), (0, 3), (1, 0), (1, 1), (1, 3), (0, 2), (1, 2)]

f32 = jnp.float32
bf16 = jnp.bfloat16


def any_spec():
    return pl.BlockSpec(memory_space=pl.ANY)


def vmem_spec():
    return pl.BlockSpec(memory_space=pltpu.VMEM)


def greet(rows, cols):
    barrier = pltpu.get_barrier_semaphore()
    for r in rows:
        pl.semaphore_signal(barrier, inc=1, device_id={"row": r}, device_id_type=MESH)
    for c in cols:
        pl.semaphore_signal(barrier, inc=1, device_id={"col": c}, device_id_type=MESH)
    pl.semaphore_wait(barrier, len(rows) + len(cols))


def remote(src, dst, send, recv, **where):
    return pltpu.make_async_remote_copy(
        src_ref=src,
        dst_ref=dst,
        send_sem=send,
        recv_sem=recv,
        device_id=where,
        device_id_type=MESH,
    )


def chip_row(me, offset, core):
    y = (me // 8 + offset[0]) % 2
    z = ((me // 2) % 4 + offset[1]) % 4
    return y * 8 + z * 2 + core


def back_chip_row(me, offset, core):
    y = (me // 8 + offset[0]) % 2
    z = ((me // 2) % 4 + 4 - offset[1]) % 4
    return y * 8 + z * 2 + core


def hidden_kernel(feat, w, hid, fchunk, buf, hbuf, a_send, a_recv, g_send, g_recv, f_send, f_recv, lsem):
    me = lax.axis_index("row")
    core = me % 2
    other = 1 - core
    partner = me - core + other
    peers = [(me + k) % NROW for k in range(1, NROW)]
    greet(peers, [])

    def piece(r):
        return feat.at[:, pl.ds(pl.multiple_of(r * CHUNK, CHUNK), CHUNK)]

    swaps = []
    for k in range(1, NROW):
        r = peers[k - 1]
        copy = remote(piece(r), buf.at[me], a_send.at[k], a_recv.at[k], row=r)
        copy.start()
        swaps.append(copy)
    mine = pltpu.make_async_copy(piece(me), buf.at[me], lsem.at[0])
    mine.start()
    mine.wait()
    for copy in swaps:
        copy.wait_recv()
    chunk_t = buf[...].astype(f32).reshape(F, CHUNK).astype(bf16)
    fchunk[...] = chunk_t
    hbuf[...] = lax.dot_general(
        chunk_t, w[...], (((0,), (0,)), ((), ())), preferred_element_type=f32
    ).astype(bf16)

    slot = hid.at[me]
    sends = []
    for k, offset in enumerate(CHIPS):
        copy = remote(hbuf, slot, g_send.at[k], g_recv.at[k], row=chip_row(me, offset, core))
        copy.start()
        sends.append(copy)
    passes = [remote(hbuf, slot, f_send.at[7], f_recv.at[7], row=partner)]
    passes[0].start()
    keep = pltpu.make_async_copy(hbuf, slot, lsem.at[1])
    keep.start()
    for k, offset in enumerate(CHIPS):
        sends[k].wait_recv()
        got = hid.at[back_chip_row(me, offset, core)]
        copy = remote(got, got, f_send.at[k], f_recv.at[k], row=partner)
        copy.start()
        passes.append(copy)
    for copy in passes:
        copy.wait()
    for copy in sends + swaps:
        copy.wait_send()
    keep.wait()


def forward_kernel(rows, cols, count, tiles, hid, out, acc):
    step = pl.program_id(0)

    @pl.when(step == 0)
    def _():
        acc[...] = jnp.zeros_like(acc)

    n = count[0]
    for t in range(STEP):
        s = step * STEP + t
        r = jnp.where(s < n, rows[s], BR)
        acc[r] += jnp.dot(tiles[0, 0, t], hid[cols[s]], preferred_element_type=f32)

    @pl.when(step == pl.num_programs(0) - 1)
    def _():
        out[...] = acc[:BR].astype(bf16)


def backward_kernel(rows, cols, count, tiles, grad_t, out, acc):
    step = pl.program_id(0)

    @pl.when(step == 0)
    def _():
        acc[...] = jnp.zeros_like(acc)

    n = count[0]
    for t in range(STEP):
        s = step * STEP + t
        c = jnp.where(s < n, cols[s], BC)
        acc[c] += jnp.dot(grad_t[rows[s]], tiles[0, 0, t], preferred_element_type=f32)

    @pl.when(step == pl.num_programs(0) - 1)
    def _():
        out[...] = acc[:BC].astype(bf16)


def middle_kernel(part, cot, act, grad_t, rbuf, gbuf, r_send, r_recv, g_send, g_recv, lsem):
    me = lax.axis_index("col")
    peers = [(me + k) % NCOL for k in range(1, NCOL)]
    greet([], peers)
    adds = []
    for q in range(SUB):
        for k in range(1, NCOL):
            c = peers[k - 1]
            copy = remote(
                part.at[c, q], rbuf.at[q, me], r_send.at[q, k], r_recv.at[q, k], col=c
            )
            copy.start()
            adds.append(copy)
    own = []
    for q in range(SUB):
        copy = pltpu.make_async_copy(part.at[me, q], rbuf.at[q, me], lsem.at[q])
        copy.start()
        own.append(copy)
    gathers = []
    keeps = []
    for q in range(SUB):
        own[q].wait()
        for k in range(1, NCOL):
            adds[q * (NCOL - 1) + k - 1].wait_recv()
        pre = jnp.sum(rbuf[q].astype(f32), axis=0)
        sig = jax.nn.sigmoid(pre)
        span = pl.ds(q * BLK, BLK)
        act[span] = (pre * sig).astype(bf16)
        grad = cot[span].astype(f32) * sig * (1.0 + pre * (1.0 - sig))
        gbuf[q] = grad.T.astype(bf16)
        slot = grad_t.at[me, q]
        for k in range(1, NCOL):
            copy = remote(gbuf.at[q], slot, g_send.at[q, k], g_recv.at[q, k], col=peers[k - 1])
            copy.start()
            gathers.append(copy)
        keep = pltpu.make_async_copy(gbuf.at[q], slot, lsem.at[SUB + q])
        keep.start()
        keeps.append(keep)
    for copy in gathers:
        copy.wait()
    for copy in adds:
        copy.wait_send()
    for copy in keeps:
        copy.wait()


def last_kernel(
    back, w, fchunk, gw, gf, obuf, pbuf, sbuf, rbuf, gfbuf, gwbuf, gwrow, gwmine, gwcol,
    p_send, p_recv, r_send, r_recv, x_send, x_recv, w_send, w_recv, c_send, c_recv, lsem,
):
    me = lax.axis_index("row")
    col = lax.axis_index("col")
    core = me % 2
    other = 1 - core
    partner = me - core + other
    peers = [(me + k) % NROW for k in range(1, NROW)]
    cpeers = [(col + k) % NCOL for k in range(1, NCOL)]
    greet(peers, cpeers)
    order = [CHIPS[6], CHIPS[5], CHIPS[3], CHIPS[4], CHIPS[2], CHIPS[0], CHIPS[1], (0, 0)]
    pairs = []
    owns = []
    for k, offset in enumerate(order):
        copy = remote(
            back.at[chip_row(me, offset, other)], pbuf.at[k], p_send.at[k], p_recv.at[k], row=partner
        )
        copy.start()
        pairs.append(copy)
        own = pltpu.make_async_copy(back.at[chip_row(me, offset, core)], obuf.at[k], lsem.at[k])
        own.start()
        owns.append(own)
    sends = []
    for k, offset in enumerate(order[:7]):
        owns[k].wait()
        pairs[k].wait_recv()
        sbuf[k] = (obuf[k].astype(f32) + pbuf[k].astype(f32)).astype(bf16)
        copy = remote(
            sbuf.at[k], rbuf.at[k], r_send.at[k], r_recv.at[k], row=chip_row(me, offset, core)
        )
        copy.start()
        sends.append(copy)
    owns[7].wait()
    pairs[7].wait_recv()
    total = obuf[7].astype(f32) + pbuf[7].astype(f32)
    for k in range(7):
        sends[k].wait_recv()
        total = total + rbuf[k].astype(f32)
    hidden_grad = total.astype(bf16)
    weight = w[...]
    gw_part = jnp.zeros((F, F), f32)
    for q in range(SUB):
        block = hidden_grad[q]
        gf_t = jnp.dot(weight, block, preferred_element_type=f32)
        gfbuf[:, :, q * BLK : (q + 1) * BLK] = gf_t.reshape(NROW, PER, BLK).astype(bf16)
        gw_part = gw_part + lax.dot_general(
            fchunk[:, q * BLK : (q + 1) * BLK],
            block,
            (((1,), (1,)), ((), ())),
            preferred_element_type=f32,
        )
    gwbuf[...] = gw_part.reshape(NROW, PER, F)
    shares = []
    for k in range(1, NROW):
        r = peers[k - 1]
        copy = remote(gwbuf.at[r], gwrow.at[k], w_send.at[k], w_recv.at[k], row=r)
        copy.start()
        shares.append(copy)
    span = pl.ds(pl.multiple_of(me * CHUNK, CHUNK), CHUNK)
    swaps = []
    for k in range(1, NROW):
        r = peers[k - 1]
        copy = remote(gfbuf.at[r], gf.at[:, span], x_send.at[k], x_recv.at[k], row=r)
        copy.start()
        swaps.append(copy)
    keep = pltpu.make_async_copy(gfbuf.at[me], gf.at[:, span], lsem.at[8])
    keep.start()
    part = gwbuf[me]
    for k in range(1, NROW):
        shares[k - 1].wait_recv()
        part = part + gwrow[k]
    gwmine[...] = part
    spreads = []
    for k in range(1, NCOL):
        copy = remote(gwmine, gwcol.at[k], c_send.at[k], c_recv.at[k], col=cpeers[k - 1])
        copy.start()
        spreads.append(copy)
    for k in range(1, NCOL):
        spreads[k - 1].wait_recv()
        part = part + gwcol[k]
    gw[...] = part
    for copy in swaps:
        copy.wait()
    for copy in pairs + sends + shares + spreads:
        copy.wait_send()
    keep.wait()


def dma(*shape):
    return pltpu.SemaphoreType.DMA(shape)


def on_device(features, weight, tiles, tile_rows, tile_cols, tile_count, cotangent):
    sds = jax.ShapeDtypeStruct
    feat_t = features.T
    rows = tile_rows.reshape(TILE_CAP)
    cols = tile_cols.reshape(TILE_CAP)
    count = tile_count.reshape(1)

    hid, fchunk = pl.pallas_call(
        hidden_kernel,
        out_shape=(sds((NROW, CHUNK, F), bf16), sds((F, CHUNK), bf16)),
        in_specs=[any_spec(), vmem_spec()],
        out_specs=(any_spec(), vmem_spec()),
        scratch_shapes=[
            pltpu.VMEM((NROW, PER, CHUNK), bf16),
            pltpu.VMEM((CHUNK, F), bf16),
            dma(NROW), dma(NROW), dma(7), dma(7), dma(8), dma(8), dma(2),
        ],
        compiler_params=pltpu.CompilerParams(
            collective_id=0, has_side_effects=True, vmem_limit_bytes=16 * MIB
        ),
        name="hidden_gather",
    )(feat_t, weight)

    def tile_block(b, *_):
        return (0, 0, b, 0, 0)

    def whole(b, *_):
        return (0, 0, 0)

    def tile_call(kernel, name, blocks_in, blocks_out, panel):
        return pl.pallas_call(
            kernel,
            out_shape=sds((blocks_out, BLK, BLK), bf16),
            grid_spec=pltpu.PrefetchScalarGridSpec(
                num_scalar_prefetch=3,
                grid=(TILE_CAP // STEP,),
                in_specs=[
                    pl.BlockSpec((1, 1, STEP, BLK, BLK), tile_block),
                    pl.BlockSpec((blocks_in, BLK, BLK), whole),
                ],
                out_specs=pl.BlockSpec((blocks_out, BLK, BLK), whole),
                scratch_shapes=[pltpu.VMEM((blocks_out + 1, BLK, BLK), f32)],
            ),
            compiler_params=pltpu.CompilerParams(vmem_limit_bytes=24 * MIB),
            cost_estimate=pl.CostEstimate(
                flops=2 * TILE_CAP * BLK**3, bytes_accessed=11 * MIB, transcendentals=0
            ),
            name=name,
        )(rows, cols, count, tiles, panel)

    part = tile_call(forward_kernel, "forward_tiles", BC, BR, hid.reshape(BC, BLK, F))

    activated, grad_t = pl.pallas_call(
        middle_kernel,
        out_shape=(sds((CHUNK, F), bf16), sds((NCOL, SUB, F, BLK), bf16)),
        in_specs=[any_spec(), vmem_spec()],
        out_specs=(vmem_spec(), any_spec()),
        scratch_shapes=[
            pltpu.VMEM((SUB, NCOL, BLK, F), bf16),
            pltpu.VMEM((SUB, F, BLK), bf16),
            dma(SUB, NCOL), dma(SUB, NCOL), dma(SUB, NCOL), dma(SUB, NCOL), dma(2 * SUB),
        ],
        compiler_params=pltpu.CompilerParams(
            collective_id=1, has_side_effects=True, vmem_limit_bytes=16 * MIB
        ),
        name="activation",
    )(part.reshape(NCOL, SUB, BLK, F), cotangent)

    back = tile_call(backward_kernel, "backward_tiles", BR, BC, grad_t.reshape(BR, F, BLK))

    grad_weight, gf_t = pl.pallas_call(
        last_kernel,
        out_shape=(sds((PER, F), f32), sds((PER, NROW * CHUNK), bf16)),
        in_specs=[any_spec(), vmem_spec(), vmem_spec()],
        out_specs=(vmem_spec(), any_spec()),
        scratch_shapes=[
            pltpu.VMEM((8, SUB, F, BLK), bf16),
            pltpu.VMEM((8, SUB, F, BLK), bf16),
            pltpu.VMEM((7, SUB, F, BLK), bf16),
            pltpu.VMEM((7, SUB, F, BLK), bf16),
            pltpu.VMEM((NROW, PER, CHUNK), bf16),
            pltpu.VMEM((NROW, PER, F), f32),
            pltpu.VMEM((NROW, PER, F), f32),
            pltpu.VMEM((PER, F), f32),
            pltpu.VMEM((NCOL, PER, F), f32),
            dma(8), dma(8), dma(7), dma(7), dma(NROW), dma(NROW), dma(NROW), dma(NROW),
            dma(NCOL), dma(NCOL), dma(9),
        ],
        compiler_params=pltpu.CompilerParams(
            collective_id=2, has_side_effects=True, vmem_limit_bytes=16 * MIB
        ),
        name="gradients",
    )(back.reshape(NROW, SUB, F, BLK), weight, fchunk)
    return (activated, grad_weight, gf_t.T)


def solution(mesh):
    return jax.shard_map(
        on_device,
        mesh=mesh,
        in_specs=(
            P("col", "row"),
            P(),
            P("row", "col", None, None, None),
            P("row", "col", None),
            P("row", "col", None),
            P("row", "col"),
            P(("row", "col"), None),
        ),
        out_specs=(P(("row", "col"), None), P("row", None), P("col", "row")),
        check_vma=False,
    )
```

time: 477 us -> 110 us (0.23)
  blocking collectives: 190 us -> 0 us
  Pallas kernels: 0 us -> 99.8 us
  waiting for transfers between devices: 88.3 us -> 0 us
  other arithmetic: 86.5 us -> 0 us
  local copies, waits for them, and re-layouts: 61.5 us -> 8.31 us
  matrix products: 34.3 us -> 0 us
  between operations: 14.8 us -> 1.37 us
    psum x3 -> x0, blocking collectives: 190 us -> none  [the longest x1 88.5 us: on_device(): summed = lax.psum(partial_panel, 'row')]
    pallas_call x0 -> x5, Pallas kernels: none -> 99.8 us  [the longest x1 29.6 us: on_device(): pl.pallas_call(middle_kernel, out_shape=(sds((CHUNK, F), bf16), sds((NCOL...]
    scatter-add x2 -> x0, other arithmetic: 84.7 us -> none  [the longest x1 51.5 us: on_device(): partial_cols = jnp.zeros((ncols, BLK, F), jnp.float32).at[local_cols].add...]
    reduce_scatter x1 -> x0, waiting for transfers between devices: 47.9 us -> none  [on_device(): pre = lax.psum_scatter(partial_rows, 'col', scatter_dimension=0, tiled=True)]
    all_gather x1 -> x0, waiting for transfers between devices: 40.4 us -> none  [on_device(): grad_rows = lax.all_gather(grad_pre, 'col', axis=0, tiled=True)]
    select_n x2 -> x0, local copies, waits for them, and re-layouts: 34.9 us -> none  [the longest x1 17.5 us: on_device(): prods = jnp.where(live[:, None, None], prods, jnp.zeros_like(prods))]
    dot_general x5 -> x0, matrix products: 34.3 us -> none  [the longest x1 15.4 us: on_device(): jnp.einsum('tji,tjf->tif', tile_set, picked_back, preferred_element_type=...]
    gather x2 -> x0, local copies, waits for them, and re-layouts: 18.4 us -> none  [the longest x1 9.83 us: on_device(): picked_back = grad_rows.reshape(BR, BLK, F)[local_rows]]
  transfers between devices with their start and end apart: 2 -> 0, of which waited for: 2 -> 0; matrix products, arithmetic and copies ran while one was open for 0% -> 0% of each run, Pallas kernels for 0% -> 0%
where the time goes in v1:
time: 110 us; the launch traced here: 109 us
  Pallas kernels  99.8 us (91%)
  local copies, waits for them, and re-layouts  8.31 us (8%)
  between operations  1.37 us (1%)
    pallas_call x1, Pallas kernels, on_device(): pl.pallas_call(middle_kernel, out_shape=(sds((CHUNK, F), bf16), sds((NCOL...  29.6 us
    pallas_call x1, Pallas kernels, on_device(): pl.pallas_call(last_kernel, out_shape=(sds((PER, F), f32), sds((PER, NROW...  29.2 us
    pallas_call x1, Pallas kernels, on_device(): pl.pallas_call(hidden_kernel, out_shape=(sds((NROW, CHUNK, F), bf16), sds...  28.8 us
    pallas_call x2, Pallas kernels, tile_call(): pl.pallas_call(kernel, out_shape=sds((blocks_out, BLK, BLK), bf16), grid_...  12.1 us
    unnamed x19, local copies, waits for them, and re-layouts  8.31 us

profile of v1, /device:TPU:0, one launch (start us, length us, event | category | flops | bytes accessed | tf_op | source)
XLA Modules:
  0.0 109.5 jit_solution(13500810077030190252)
XLA Ops:
  1.3 0.0 copy-start.2
  1.3 0.7 copy-done.2
  2.0 0.0 copy-start.5
  2.0 0.9 copy-done.5
  2.9 28.8 %hidden_gather.1 = (bf16[16,512,128]{2,1,0:T(8,128)(2,1)S(1)}, bf16[128,512]{1,0:T(8,128)(2,1)S(1)}) custom-call(bf16[8,8192]{1,0:T(8,128)(2,1)S(1)} %bitcast.15, bf16[128,128]{1,0:T(8,128)(2,1)S(1)} %copy-done.2), custom_call_target="tpu_custom_call" | custom-call | tf_op jit(solution)/shard_map/hidden_gather/pallas_call | solution.py:303
  31.8 0.0 copy-start
  31.8 3.4 %copy-done = bf16[1,1,256,128,128]{4,3,2,1,0:T(8,128)(2,1)S(1)} copy-done((bf16[1,1,256,128,128]{4,3,2,1,0:T(8,128)(2,1)S(1)}, bf16[1,1,256,128,128]{4,3,2,1,0:T(8,128)(2,1)}, u32[]{:S(2)}) %copy-start) | copy-done | bytes 8388632
  35.2 0.0 copy-start.6
  35.2 0.7 copy-done.6
  35.9 0.0 copy-start.7
  35.9 0.7 copy-done.7
  36.5 0.0 copy-start.4
  36.5 0.0 copy-start.1
  36.5 6.1 %forward_tiles.1 = bf16[32,128,128]{2,1,0:T(8,128)(2,1)S(1)} custom-call(s32[256]{0:T(256)S(1)} %bitcast.17, s32[256]{0:T(256)S(1)} %bitcast.19, s32[1]{0:T(128)} %bitcast.9.count, bf16[1,1,256,128,128]{4,3,2,1,0:T(8,128)(2,1)S(1)} %copy-done, bf16[64,128,128]{2,1,0:T(8,128)(2,1)S(1)} %bitcast.13), custom_call_target="tpu_custom_call" | custom-call | flops 1073741824 | bytes 11534336 | tf_op jit(solution)/shard_map/forward_tiles/pallas_call | solution.py:326
  42.6 0.0 copy-done.4
  42.6 29.6 %activation.1 = (bf16[512,128]{1,0:T(8,128)(2,1)S(1)}, bf16[8,4,128,128]{3,2,1,0:T(8,128)(2,1)S(1)}) custom-call(bf16[8,4,128,128]{3,2,1,0:T(8,128)(2,1)S(1)} %bitcast.12, bf16[512,128]{1,0:T(8,128)(2,1)S(1)} %copy-done.4), custom_call_target="tpu_custom_call" | custom-call | tf_op jit(solution)/shard_map/activation/pallas_call | solution.py:348
  72.2 0.0 copy-done.1
  72.2 0.0 copy-start.3
  72.3 6.1 %backward_tiles.1 = bf16[64,128,128]{2,1,0:T(8,128)(2,1)S(1)} custom-call(s32[256]{0:T(256)S(1)} %bitcast.18, s32[256]{0:T(256)S(1)} %bitcast.20, s32[1]{0:T(128)} %bitcast.10.count, bf16[1,1,256,128,128]{4,3,2,1,0:T(8,128)(2,1)S(1)} %copy-done.1, bf16[32,128,128]{2,1,0:T(8,128)(2,1)S(1)} %bitcast.14), custom_call_target="tpu_custom_call" | custom-call | flops 1073741824 | bytes 11534336 | tf_op jit(solution)/shard_map/backward_tiles/pallas_call | solution.py:326
  78.3 0.0 copy-done.3
  78.3 29.2 %gradients.1 = (f32[8,128]{1,0:T(8,128)S(1)}, bf16[8,8192]{1,0:T(8,128)(2,1)S(1)}) custom-call(bf16[16,4,128,128]{3,2,1,0:T(8,128)(2,1)S(1)} %bitcast.11, bf16[128,128]{1,0:T(8,128)(2,1)S(1)} %copy-done.3, bf16[128,512]{1,0:T(8,128)(2,1)S(1)} %get-tuple-element.12.fchunk), custom_call_target="tpu_custom_call" | custom-call | tf_op jit(solution)/shard_map/gradients/pallas_call | solution.py:366
  107.6 0.7 copy.14
  108.2 0.6 copy.15
  108.8 0.7 copy.16
Async XLA Ops:
  1.3 0.8 copy-start.2
  2.0 0.9 copy-start.5
  31.8 3.4 %copy-start = (bf16[1,1,256,128,128]{4,3,2,1,0:T(8,128)(2,1)S(1)}, bf16[1,1,256,128,128]{4,3,2,1,0:T(8,128)(2,1)}, u32[]{:S(2)}) copy-start(bf16[1,1,256,128,128]{4,3,2,1,0:T(8,128)(2,1)} %tiles.3) | copy-start | bytes 25165828
  35.2 0.7 copy-start.6
  35.9 0.7 copy-start.7
  36.5 6.1 %copy-start.4 = (bf16[512,128]{1,0:T(8,128)(2,1)S(1)}, bf16[512,128]{1,0:T(8,128)(2,1)}, u32[]{:S(2)}) copy-start(bf16[512,128]{1,0:T(8,128)(2,1)} %cot.1) | copy-start | bytes 393220
  36.5 35.7 %copy-start.1 = (bf16[1,1,256,128,128]{4,3,2,1,0:T(8,128)(2,1)S(1)}, bf16[1,1,256,128,128]{4,3,2,1,0:T(8,128)(2,1)}, u32[]{:S(2)}) copy-start(bf16[1,1,256,128,128]{4,3,2,1,0:T(8,128)(2,1)} %tiles.3) | copy-start | bytes 25165828
  72.2 6.1 %copy-start.3 = (bf16[128,128]{1,0:T(8,128)(2,1)S(1)}, bf16[128,128]{1,0:T(8,128)(2,1)}, u32[]{:S(2)}) copy-start(bf16[128,128]{1,0:T(8,128)(2,1)} %w.3) | copy-start | bytes 98308

commit v2 on v0

v2 whole, which is shorter than its diff:
```python
import jax
import jax.numpy as jnp
from jax import lax
from jax.experimental import pallas as pl
from jax.experimental.pallas import tpu as pltpu
from jax.sharding import PartitionSpec as P

F = 128
BLK = 128
NROW = 16
NCOL = 8
BR = 32
BC = 64
TILE_CAP = 256
PANEL = BC * BLK
HALF = PANEL // 2
CHUNK = 512
SUB = CHUNK // BLK
PER = F // NROW
UNROLL = 32
MIB = 1024 * 1024
MESH = pl.DeviceIdType.MESH

f32 = jnp.float32
bf16 = jnp.bfloat16
i32 = jnp.int32

ORDER, TAKE, KEEP, LAST, HAS = range(5)


def any_spec():
    return pl.BlockSpec(memory_space=pl.ANY)


def vmem_spec():
    return pl.BlockSpec(memory_space=pltpu.VMEM)


def remote(src, dst, send, recv, **where):
    return pltpu.make_async_remote_copy(
        src_ref=src,
        dst_ref=dst,
        send_sem=send,
        recv_sem=recv,
        device_id=where,
        device_id_type=MESH,
    )


def make_plan(key_block, take, live, dead_block):
    n = TILE_CAP
    across = lax.broadcasted_iota(i32, (n, n), 1)
    down = lax.broadcasted_iota(i32, (n, n), 0)
    block = jnp.where(live, key_block, dead_block)
    block_r = jnp.broadcast_to(block, (n, n))
    block_c = block_r.T
    key_r = block_r * n + across
    key_c = block_c * n + down
    rank = jnp.sum(jnp.where(key_c < key_r, 1, 0), axis=0, keepdims=True)
    rank_c = jnp.broadcast_to(rank, (n, n)).T
    take_c = jnp.broadcast_to(take, (n, n)).T
    hit = rank_c == across
    order = jnp.sum(jnp.where(hit, down, 0), axis=0, keepdims=True)
    taken = jnp.sum(jnp.where(hit, take_c, 0), axis=0, keepdims=True)
    mine = jnp.sum(jnp.where(hit, block_c, 0), axis=0, keepdims=True)
    before = jnp.sum(jnp.where(rank_c == across - 1, block_c, 0), axis=0, keepdims=True)
    first = lax.broadcasted_iota(i32, (1, n), 1) == 0
    keep = jnp.where(first | (mine != before), 0, 1)
    last = jnp.maximum(jnp.sum(jnp.where(block_c <= across, 1, 0), axis=0, keepdims=True) - 1, 0)
    has = jnp.where(jnp.sum(jnp.where(block_c == across, 1, 0), axis=0, keepdims=True) > 0, 1, 0)
    return [order, taken, keep, last, has]


def layer_kernel(
    feat_in, weight, tiles, tile_rows, tile_cols, tile_count, cot,
    act, gw, gf,
    tv, feat, hid, prods, part, pbuf_col, gbuf, grad_t, back, pbuf, sbuf, rbuf,
    gfbuf, gwbuf, gwrow, gwmine, gwcol, plan_v, plan_s,
    l_sem, a_send, a_recv, f_send, f_recv, r_send, r_recv, g_send, g_recv,
    p_send, p_recv, s_send, s_recv, x_send, x_recv, w_send, w_recv, c_send, c_recv,
):
    me = lax.axis_index("row")
    col = lax.axis_index("col")
    yh = me // 8
    z = (me // 2) % 4
    core = me % 2
    other = 1 - core

    def at(dy, dz, k):
        return ((yh + dy) % 2) * 8 + ((z + dz) % 4) * 2 + k

    partner = at(0, 0, other)
    up, down, across = at(0, 1, core), at(0, 3, core), at(1, 0, core)
    peers = [(me + k) % NROW for k in range(1, NROW)]
    cpeers = [(col + k) % NCOL for k in range(1, NCOL)]

    tile_copy = pltpu.make_async_copy(tiles.at[0, 0], tv, l_sem.at[0])
    tile_copy.start()
    own_copy = pltpu.make_async_copy(feat_in, feat.at[me], l_sem.at[1])
    own_copy.start()

    barrier = pltpu.get_barrier_semaphore()
    for r in peers:
        pl.semaphore_signal(barrier, inc=1, device_id={"row": r}, device_id_type=MESH)
    for c in cpeers:
        pl.semaphore_signal(barrier, inc=1, device_id={"col": c}, device_id_type=MESH)
    pl.semaphore_wait(barrier, len(peers) + len(cpeers))

    started = []

    def half(ref, h):
        return ref.at[:, pl.ds(h * HALF, HALF)]

    def send(src, slab, h, index, to):
        dst = feat.at[slab] if h is None else half(feat.at[slab], h)
        copy = remote(src, dst, a_send.at[index], a_recv.at[index], row=to)
        copy.start()
        started.append(copy)
        return copy

    def pass_on(slab, h, index, to):
        return send(half(feat.at[slab], h), slab, h, index, to)

    got = {}
    got["d", 0] = send(half(feat_in, 0), me, 0, 0, up)
    got["u", 1] = send(half(feat_in, 1), me, 1, 3, down)
    got["y", 0] = send(half(feat_in, 0), me, 0, 4, across)
    got["y", 1] = send(half(feat_in, 1), me, 1, 5, across)
    got["d", 1] = send(half(feat_in, 1), me, 1, 1, up)
    got["u", 0] = send(half(feat_in, 0), me, 0, 2, down)
    got["c", 2] = send(feat_in, me, None, 6, partner)

    live = lax.broadcasted_iota(i32, (1, TILE_CAP), 1) < tile_count[0, 0]
    forward = make_plan(tile_rows[0], tile_cols[0], live, BR)
    backward = make_plan(tile_cols[0], tile_rows[0], live, BC)
    for i, line in enumerate(forward + backward):
        plan_v[i : i + 1, :] = line
    plan_copy = pltpu.make_async_copy(plan_v, plan_s, l_sem.at[2])
    plan_copy.start()

    handed = []

    def hand(slab, h):
        index = len(handed)
        piece = half(feat.at[slab], h)
        copy = remote(piece, piece, f_send.at[index], f_recv.at[index], row=partner)
        copy.start()
        handed.append(copy)

    below, above = at(0, 3, core), at(0, 1, core)
    far = at(0, 2, core)
    y_own, y_below, y_above, y_far = (at(1, d, core) for d in (0, 3, 1, 2))

    got["d", 0].wait_recv()
    got["far", 0] = pass_on(below, 0, 7, up)
    hand(below, 0)
    got["u", 1].wait_recv()
    got["far", 1] = pass_on(above, 1, 8, down)
    hand(above, 1)
    got["y", 0].wait_recv()
    got["yd", 0] = pass_on(y_own, 0, 9, up)
    got["y", 1].wait_recv()
    got["yu", 1] = pass_on(y_own, 1, 12, down)
    got["yd", 1] = pass_on(y_own, 1, 10, up)
    got["yu", 0] = pass_on(y_own, 0, 11, down)
    hand(y_own, 0)
    hand(y_own, 1)
    got["d", 1].wait_recv()
    hand(below, 1)
    got["u", 0].wait_recv()
    hand(above, 0)
    got["far", 0].wait_recv()
    hand(far, 0)
    got["far", 1].wait_recv()
    hand(far, 1)
    got["yd", 0].wait_recv()
    got["yfar", 0] = pass_on(y_below, 0, 13, up)
    got["yu", 1].wait_recv()
    got["yfar", 1] = pass_on(y_above, 1, 14, down)
    hand(y_below, 0)
    hand(y_above, 1)
    got["yd", 1].wait_recv()
    hand(y_below, 1)
    got["yu", 0].wait_recv()
    hand(y_above, 0)
    got["yfar", 0].wait_recv()
    hand(y_far, 0)
    got["yfar", 1].wait_recv()
    hand(y_far, 1)
    got["c", 2].wait_recv()
    own_copy.wait()
    for copy in handed:
        copy.wait_recv()

    def columns(start, width):
        span = pl.ds(pl.multiple_of(start, BLK), width)
        return feat[:, :, span].astype(f32).reshape(F, width).astype(bf16)

    w = weight[...]

    def hidden_step(i, carry):
        for t in range(8):
            b = i * 8 + t
            hid[b] = lax.dot_general(
                columns(b * BLK, BLK), w, (((0,), (0,)), ((), ())), preferred_element_type=f32
            ).astype(bf16)
        return carry

    lax.fori_loop(0, BC // 8, hidden_step, 0)

    plan_copy.wait()
    tile_copy.wait()

    def forward_step(i, total):
        for t in range(UNROLL):
            p = i * UNROLL + t
            keep = plan_s[KEEP, p].astype(f32)
            total = total * keep + jnp.dot(
                tv[plan_s[ORDER, p]], hid[plan_s[TAKE, p]], preferred_element_type=f32
            )
            prods[p] = total.astype(bf16)
        return total

    lax.fori_loop(0, TILE_CAP // UNROLL, forward_step, jnp.zeros((BLK, F), f32))
    for b in range(BR):
        has = plan_s[HAS, b].astype(f32)
        part[b // SUB, b % SUB] = (prods[plan_s[LAST, b]].astype(f32) * has).astype(bf16)

    adds = []
    for q in range(SUB):
        for k in range(1, NCOL):
            c = cpeers[k - 1]
            copy = remote(
                part.at[c, q], pbuf_col.at[q, k], r_send.at[q, k], r_recv.at[q, k], col=c
            )
            copy.start()
            adds.append(copy)
    gathers = []
    for q in range(SUB):
        pre = part[col, q].astype(f32)
        for k in range(1, NCOL):
            adds[q * (NCOL - 1) + k - 1].wait_recv()
            pre = pre + pbuf_col[q, k].astype(f32)
        sig = jax.nn.sigmoid(pre)
        span = pl.ds(q * BLK, BLK)
        act[span] = (pre * sig).astype(bf16)
        grad = cot[span].astype(f32) * sig * (1.0 + pre * (1.0 - sig))
        grad_block = grad.T.astype(bf16)
        gbuf[q] = grad_block
        grad_t[col * SUB + q] = grad_block
        slot = grad_t.at[col * SUB + q]
        for k in range(1, NCOL):
            copy = remote(gbuf.at[q], slot, g_send.at[q, k], g_recv.at[q, k], col=cpeers[k - 1])
            copy.start()
            gathers.append(copy)
    for copy in gathers:
        copy.wait_recv()

    def backward_step(i, total):
        for t in range(UNROLL):
            p = i * UNROLL + t
            keep = plan_s[5 + KEEP, p].astype(f32)
            total = total * keep + jnp.dot(
                grad_t[plan_s[5 + TAKE, p]], tv[plan_s[5 + ORDER, p]], preferred_element_type=f32
            )
            prods[p] = total.astype(bf16)
        return total

    lax.fori_loop(0, TILE_CAP // UNROLL, backward_step, jnp.zeros((F, BLK), f32))
    for b in range(BC):
        has = plan_s[5 + HAS, b].astype(f32)
        back[b // SUB, b % SUB] = (prods[plan_s[5 + LAST, b]].astype(f32) * has).astype(bf16)

    order = [(1, 2), (0, 2), (1, 1), (1, 3), (1, 0), (0, 1), (0, 3), (0, 0)]
    pairs = []
    for k, (dy, dz) in enumerate(order):
        copy = remote(
            back.at[at(dy, dz, other)], pbuf.at[k], p_send.at[k], p_recv.at[k], row=partner
        )
        copy.start()
        pairs.append(copy)
    sums = []
    for k, (dy, dz) in enumerate(order[:7]):
        pairs[k].wait_recv()
        sbuf[k] = (back[at(dy, dz, core)].astype(f32) + pbuf[k].astype(f32)).astype(bf16)
        copy = remote(sbuf.at[k], rbuf.at[k], s_send.at[k], s_recv.at[k], row=at(dy, dz, core))
        copy.start()
        sums.append(copy)
    feat_chunk = columns(me * CHUNK, CHUNK)
    pairs[7].wait_recv()
    for copy in sums:
        copy.wait_recv()
    gw_part = jnp.zeros((F, F), f32)
    for q in range(SUB):
        total = back[me, q].astype(f32) + pbuf[7, q].astype(f32)
        for k in range(7):
            total = total + rbuf[k, q].astype(f32)
        block = total.astype(bf16)
        gf_t = jnp.dot(w, block, preferred_element_type=f32)
        gfbuf[:, :, q * BLK : (q + 1) * BLK] = gf_t.reshape(NROW, PER, BLK).astype(bf16)
        gw_part = gw_part + lax.dot_general(
            feat_chunk[:, q * BLK : (q + 1) * BLK],
            block,
            (((1,), (1,)), ((), ())),
            preferred_element_type=f32,
        )
    gwbuf[...] = gw_part.reshape(NROW, PER, F)

    shares = []
    for k in range(1, NROW):
        r = peers[k - 1]
        copy = remote(gwbuf.at[r], gwrow.at[k], w_send.at[k], w_recv.at[k], row=r)
        copy.start()
        shares.append(copy)
    place = pl.ds(pl.multiple_of(me * CHUNK, CHUNK), CHUNK)
    swaps = []
    for k in range(1, NROW):
        r = peers[k - 1]
        copy = remote(gfbuf.at[r], gf.at[:, place], x_send.at[k], x_recv.at[k], row=r)
        copy.start()
        swaps.append(copy)
    gf[:, place] = gfbuf[me]
    gw_sum = gwbuf[me]
    for k in range(1, NROW):
        shares[k - 1].wait_recv()
        gw_sum = gw_sum + gwrow[k]
    gwmine[...] = gw_sum
    spreads = []
    for k in range(1, NCOL):
        copy = remote(gwmine, gwcol.at[k], c_send.at[k], c_recv.at[k], col=cpeers[k - 1])
        copy.start()
        spreads.append(copy)
    for k in range(1, NCOL):
        spreads[k - 1].wait_recv()
        gw_sum = gw_sum + gwcol[k]
    gw[...] = gw_sum
    for copy in swaps:
        copy.wait()
    for copy in started + handed + adds + gathers + pairs + sums + shares + spreads:
        copy.wait_send()


def dma(*shape):
    return pltpu.SemaphoreType.DMA(shape)


def on_device(features, weight, tiles, tile_rows, tile_cols, tile_count, cotangent):
    sds = jax.ShapeDtypeStruct
    activated, grad_weight, gf_t = pl.pallas_call(
        layer_kernel,
        out_shape=(sds((CHUNK, F), bf16), sds((PER, F), f32), sds((PER, PANEL), bf16)),
        in_specs=[
            any_spec(), vmem_spec(), any_spec(), vmem_spec(), vmem_spec(), vmem_spec(), vmem_spec(),
        ],
        out_specs=(vmem_spec(), vmem_spec(), vmem_spec()),
        scratch_shapes=[
            pltpu.VMEM((TILE_CAP, BLK, BLK), bf16),
            pltpu.VMEM((NROW, PER, PANEL), bf16),
            pltpu.VMEM((BC, BLK, F), bf16),
            pltpu.VMEM((TILE_CAP, BLK, BLK), bf16),
            pltpu.VMEM((NCOL, SUB, BLK, F), bf16),
            pltpu.VMEM((SUB, NCOL, BLK, F), bf16),
            pltpu.VMEM((SUB, F, BLK), bf16),
            pltpu.VMEM((BR, F, BLK), bf16),
            pltpu.VMEM((NROW, SUB, F, BLK), bf16),
            pltpu.VMEM((8, SUB, F, BLK), bf16),
            pltpu.VMEM((7, SUB, F, BLK), bf16),
            pltpu.VMEM((7, SUB, F, BLK), bf16),
            pltpu.VMEM((NROW, PER, CHUNK), bf16),
            pltpu.VMEM((NROW, PER, F), f32),
            pltpu.VMEM((NROW, PER, F), f32),
            pltpu.VMEM((PER, F), f32),
            pltpu.VMEM((NCOL, PER, F), f32),
            pltpu.VMEM((16, TILE_CAP), i32),
            pltpu.SMEM((16, TILE_CAP), i32),
            dma(3), dma(15), dma(15), dma(14), dma(14),
            dma(SUB, NCOL), dma(SUB, NCOL), dma(SUB, NCOL), dma(SUB, NCOL),
            dma(8), dma(8), dma(7), dma(7), dma(NROW), dma(NROW), dma(NROW), dma(NROW),
            dma(NCOL), dma(NCOL),
        ],
        compiler_params=pltpu.CompilerParams(
            collective_id=0, has_side_effects=True, vmem_limit_bytes=48 * MIB
        ),
        cost_estimate=pl.CostEstimate(
            flops=4 * TILE_CAP * BLK**3, bytes_accessed=11 * MIB, transcendentals=CHUNK * F
        ),
        name="graph_layer",
    )(features.T, weight, tiles, tile_rows[0], tile_cols[0], tile_count, cotangent)
    return (activated, grad_weight, gf_t.T)


def solution(mesh):
    return jax.shard_map(
        on_device,
        mesh=mesh,
        in_specs=(
            P("col", "row"),
            P(),
            P("row", "col", None, None, None),
            P("row", "col", None),
            P("row", "col", None),
            P("row", "col"),
            P(("row", "col"), None),
        ),
        out_specs=(P(("row", "col"), None), P("row", None), P("col", "row")),
        check_vma=False,
    )
```

time: 477 us -> 90.7 us (0.19)
  blocking collectives: 190 us -> 0 us
  waiting for transfers between devices: 88.3 us -> 0 us
  other arithmetic: 86.5 us -> 0 us
  Pallas kernels: 0 us -> 83.2 us
  local copies, waits for them, and re-layouts: 61.5 us -> 5.82 us
  matrix products: 34.3 us -> 0 us
  between operations: 14.8 us -> 1.3 us
    psum x3 -> x0, blocking collectives: 190 us -> none  [the longest x1 88.5 us: on_device(): summed = lax.psum(partial_panel, 'row')]
    scatter-add x2 -> x0, other arithmetic: 84.7 us -> none  [the longest x1 51.5 us: on_device(): partial_cols = jnp.zeros((ncols, BLK, F), jnp.float32).at[local_cols].add...]
    pallas_call x0 -> x1, Pallas kernels: none -> 83.2 us  [on_device(): pl.pallas_call(layer_kernel, out_shape=(sds((CHUNK, F), bf16), sds((PER,...]
    reduce_scatter x1 -> x0, waiting for transfers between devices: 47.9 us -> none  [on_device(): pre = lax.psum_scatter(partial_rows, 'col', scatter_dimension=0, tiled=True)]
    all_gather x1 -> x0, waiting for transfers between devices: 40.4 us -> none  [on_device(): grad_rows = lax.all_gather(grad_pre, 'col', axis=0, tiled=True)]
    select_n x2 -> x0, local copies, waits for them, and re-layouts: 34.9 us -> none  [the longest x1 17.5 us: on_device(): prods = jnp.where(live[:, None, None], prods, jnp.zeros_like(prods))]
    dot_general x5 -> x0, matrix products: 34.3 us -> none  [the longest x1 15.4 us: on_device(): jnp.einsum('tji,tjf->tif', tile_set, picked_back, preferred_element_type=...]
    gather x2 -> x0, local copies, waits for them, and re-layouts: 18.4 us -> none  [the longest x1 9.83 us: on_device(): picked_back = grad_rows.reshape(BR, BLK, F)[local_rows]]
  transfers between devices with their start and end apart: 2 -> 0, of which waited for: 2 -> 0; matrix products, arithmetic and copies ran while one was open for 0% -> 0% of each run, Pallas kernels for 0% -> 0%
where the time goes in v2:
time: 90.7 us; the launch traced here: 90.3 us
  Pallas kernels  83.2 us (92%)
  local copies, waits for them, and re-layouts  5.82 us (6%)
  between operations  1.3 us (1%)
    pallas_call x1, Pallas kernels, on_device(): pl.pallas_call(layer_kernel, out_shape=(sds((CHUNK, F), bf16), sds((PER,...  83.2 us
    unnamed x13, local copies, waits for them, and re-layouts  5.82 us

profile of v2, /device:TPU:0, one launch (start us, length us, event | category | flops | bytes accessed | tf_op | source)
XLA Modules:
  0.0 90.3 jit_solution(3530895308126173801)
XLA Ops:
  1.3 0.0 copy-start
  1.3 0.9 copy-done
  2.2 0.0 copy-start.1
  2.2 0.9 copy-done.1
  3.1 0.0 copy-start.2
  3.1 0.8 copy-done.2
  3.8 0.0 copy-start.3
  3.8 0.7 copy-done.3
  4.5 0.0 copy-start.4
  4.5 0.7 copy-done.4
  5.2 83.2 %graph_layer.1 = (bf16[512,128]{1,0:T(8,128)(2,1)S(1)}, f32[8,128]{1,0:T(8,128)S(1)}, bf16[8,8192]{1,0:T(8,128)(2,1)S(1)}) custom-call(bf16[8,8192]{1,0:T(8,128)(2,1)S(1)} %bitcast.4, bf16[128,128]{1,0:T(8,128)(2,1)S(1)} %copy-done.2, bf16[1,1,256,128,128]{4,3,2,1,0:T(8,128)(2,1)} %tiles.1, s32[1,256]{1,0:T(1,128)S(1)} %bitcast.6, s32[1,256]{1,0:T(1,128)S(1)} %bitcast.7, ...), custom_call_target="tpu_custom_call" | custom-call | flops 2147483648 | bytes 11534336 | tf_op jit(solution)/shard_map/graph_layer/pallas_call | solution.py:349
  88.4 0.7 copy.14
  89.0 0.6 copy.15
  89.6 0.7 copy.16
Async XLA Ops:
  1.3 0.9 %copy-start = (bf16[8192,8]{0,1:T(8,128)(2,1)S(1)}, bf16[8192,8]{0,1:T(8,128)(2,1)}, u32[]{:S(2)}) copy-start(bf16[8192,8]{0,1:T(8,128)(2,1)} %param.7) | copy-start | bytes 393220
  2.2 0.9 %copy-start.1 = (bf16[512,128]{1,0:T(8,128)(2,1)S(1)}, bf16[512,128]{1,0:T(8,128)(2,1)}, u32[]{:S(2)}) copy-start(bf16[512,128]{1,0:T(8,128)(2,1)} %cot.1) | copy-start | bytes 393220
  3.1 0.8 copy-start.2
  3.8 0.7 copy-start.3
  4.5 0.7 copy-start.4

commit v3 on v2

v3 whole, which is shorter than its diff:
```python
import jax
import jax.numpy as jnp
from jax import lax
from jax.experimental import pallas as pl
from jax.experimental.pallas import tpu as pltpu
from jax.sharding import PartitionSpec as P

F = 128
BLK = 128
NROW = 16
NCOL = 8
BR = 32
BC = 64
TILE_CAP = 256
PANEL = BC * BLK
HALF = PANEL // 2
CHUNK = 512
SUB = CHUNK // BLK
PER = F // NROW
UNROLL = 32
MIB = 1024 * 1024
MESH = pl.DeviceIdType.MESH

f32 = jnp.float32
bf16 = jnp.bfloat16
i32 = jnp.int32

ORDER, TAKE, KEEP, LAST, HAS = range(5)


def any_spec():
    return pl.BlockSpec(memory_space=pl.ANY)


def vmem_spec():
    return pl.BlockSpec(memory_space=pltpu.VMEM)


def start_remote(pending, src, dst, send, recv, **where):
    copy = pltpu.make_async_remote_copy(
        src_ref=src,
        dst_ref=dst,
        send_sem=send,
        recv_sem=recv,
        device_id=where,
        device_id_type=MESH,
    )
    copy.start()
    pending.append(copy)
    return copy


def make_plan(key_block, take, live, dead_block):
    n = TILE_CAP
    across = lax.broadcasted_iota(i32, (n, n), 1)
    down = lax.broadcasted_iota(i32, (n, n), 0)
    block = jnp.where(live, key_block, dead_block)
    block_r = jnp.broadcast_to(block, (n, n))
    block_c = block_r.T
    key_r = block_r * n + across
    key_c = block_c * n + down
    rank = jnp.sum(jnp.where(key_c < key_r, 1, 0), axis=0, keepdims=True)
    rank_c = jnp.broadcast_to(rank, (n, n)).T
    take_c = jnp.broadcast_to(take, (n, n)).T
    hit = rank_c == across
    order = jnp.sum(jnp.where(hit, down, 0), axis=0, keepdims=True)
    taken = jnp.sum(jnp.where(hit, take_c, 0), axis=0, keepdims=True)
    mine = jnp.sum(jnp.where(hit, block_c, 0), axis=0, keepdims=True)
    before = jnp.sum(jnp.where(rank_c == across - 1, block_c, 0), axis=0, keepdims=True)
    first = lax.broadcasted_iota(i32, (1, n), 1) == 0
    keep = jnp.where(first | (mine != before), 0, 1)
    last = jnp.maximum(jnp.sum(jnp.where(block_c <= across, 1, 0), axis=0, keepdims=True) - 1, 0)
    has = jnp.where(jnp.sum(jnp.where(block_c == across, 1, 0), axis=0, keepdims=True) > 0, 1, 0)
    return [order, taken, keep, last, has]


def layer_kernel(
    feat_in, weight_in, tiles, rows_in, cols_in, count_in, cot_in,
    act, gw, gf,
    weight, rows_v, cols_v, count_v, cot,
    tv, feat, hid, prods, part, x_far, x_sum, x_below, x_above, y_sum, y_got, mine, grad_t,
    back, slabs, pbuf, sbuf, rbuf, gwbuf, gwpair, gwsum, gwrow, gwmine, gwcol, plan_v, plan_s,
    l_sem, a_send, a_recv, f_send, f_recv, r_send, r_recv, g_send, g_recv,
    p_send, p_recv, s_send, s_recv, w_send, w_recv, c_send, c_recv,
):
    me = lax.axis_index("row")
    col = lax.axis_index("col")
    yh = me // 8
    z = (me // 2) % 4
    core = me % 2
    other = 1 - core

    def at(dy, dz, k):
        return ((yh + dy) % 2) * 8 + ((z + dz) % 4) * 2 + k

    partner = at(0, 0, other)
    up, down, across = at(0, 1, core), at(0, 3, core), at(1, 0, core)
    peers = [partner] + [at(dy, dz, core) for dy in (0, 1) for dz in range(4) if dy + dz]
    cpeers = [(col + k) % NCOL for k in range(1, NCOL)]

    tile_copy = pltpu.make_async_copy(tiles.at[0, 0], tv, l_sem.at[0])
    tile_copy.start()
    own_copy = pltpu.make_async_copy(feat_in, feat.at[me], l_sem.at[1])
    own_copy.start()
    small = []
    for i, (src, dst) in enumerate(
        [(rows_in, rows_v), (cols_in, cols_v), (count_in, count_v), (weight_in, weight), (cot_in, cot)]
    ):
        copy = pltpu.make_async_copy(src, dst, l_sem.at[3 + i])
        copy.start()
        small.append(copy)

    barrier = pltpu.get_barrier_semaphore()
    for r in peers:
        pl.semaphore_signal(barrier, inc=1, device_id={"row": r}, device_id_type=MESH)
    for c in cpeers:
        pl.semaphore_signal(barrier, inc=1, device_id={"col": c}, device_id_type=MESH)
    pl.semaphore_wait(barrier, len(peers) + len(cpeers))

    pending = []

    def half(ref, h):
        return ref.at[:, pl.ds(h * HALF, HALF)]

    def send(src, slab, h, index, to):
        dst = feat.at[slab] if h is None else half(feat.at[slab], h)
        copy = start_remote(pending, src, dst, a_send.at[index], a_recv.at[index], row=to)
        return copy

    def pass_on(slab, h, index, to):
        return send(half(feat.at[slab], h), slab, h, index, to)

    got = {}
    got["d", 0] = send(half(feat_in, 0), me, 0, 0, up)
    got["u", 1] = send(half(feat_in, 1), me, 1, 3, down)
    got["y", 0] = send(half(feat_in, 0), me, 0, 4, across)
    got["y", 1] = send(half(feat_in, 1), me, 1, 5, across)
    got["d", 1] = send(half(feat_in, 1), me, 1, 1, up)
    got["u", 0] = send(half(feat_in, 0), me, 0, 2, down)
    got["c", 2] = send(feat_in, me, None, 6, partner)

    for copy in small:
        copy.wait()
    live = lax.broadcasted_iota(i32, (1, TILE_CAP), 1) < count_v[0, 0]
    forward = make_plan(rows_v[...], cols_v[...], live, BR)
    backward = make_plan(cols_v[...], rows_v[...], live, BC)
    for i, line in enumerate(forward + backward):
        plan_v[i : i + 1, :] = line
    plan_copy = pltpu.make_async_copy(plan_v, plan_s, l_sem.at[2])
    plan_copy.start()

    handed = []

    def hand(slab, h):
        index = len(handed)
        piece = half(feat.at[slab], h)
        copy = start_remote(pending, piece, piece, f_send.at[index], f_recv.at[index], row=partner)
        handed.append(copy)

    below, above = at(0, 3, core), at(0, 1, core)
    far = at(0, 2, core)
    y_own, y_below, y_above, y_far = (at(1, d, core) for d in (0, 3, 1, 2))

    got["d", 0].wait_recv()
    got["far", 0] = pass_on(below, 0, 7, up)
    hand(below, 0)
    got["u", 1].wait_recv()
    got["far", 1] = pass_on(above, 1, 8, down)
    hand(above, 1)
    got["y", 0].wait_recv()
    got["yd", 0] = pass_on(y_own, 0, 9, up)
    got["y", 1].wait_recv()
    got["yu", 1] = pass_on(y_own, 1, 12, down)
    got["yd", 1] = pass_on(y_own, 1, 10, up)
    got["yu", 0] = pass_on(y_own, 0, 11, down)
    hand(y_own, 0)
    hand(y_own, 1)
    got["d", 1].wait_recv()
    hand(below, 1)
    got["u", 0].wait_recv()
    hand(above, 0)
    got["far", 0].wait_recv()
    got["yfar", 0] = pass_on(far, 0, 13, across)
    hand(far, 0)
    got["far", 1].wait_recv()
    got["yfar", 1] = pass_on(far, 1, 14, across)
    hand(far, 1)
    got["yd", 0].wait_recv()
    hand(y_below, 0)
    got["yu", 1].wait_recv()
    hand(y_above, 1)
    got["yd", 1].wait_recv()
    hand(y_below, 1)
    got["yu", 0].wait_recv()
    hand(y_above, 0)
    got["yfar", 0].wait_recv()
    hand(y_far, 0)
    got["yfar", 1].wait_recv()
    hand(y_far, 1)
    got["c", 2].wait_recv()
    own_copy.wait()
    for copy in handed:
        copy.wait_recv()

    def columns(start, width):
        span = pl.ds(pl.multiple_of(start, BLK), width)
        return feat[:, :, span].astype(f32).reshape(F, width).astype(bf16)

    w = weight[...]

    def hidden_step(i, carry):
        for t in range(8):
            b = i * 8 + t
            hid[b] = lax.dot_general(
                columns(b * BLK, BLK), w, (((0,), (0,)), ((), ())), preferred_element_type=f32
            ).astype(bf16)
        return carry

    lax.fori_loop(0, BC // 8, hidden_step, 0)

    plan_copy.wait()
    tile_copy.wait()

    def forward_step(i, total):
        for t in range(UNROLL):
            p = i * UNROLL + t
            keep = plan_s[KEEP, p].astype(f32)
            total = total * keep + jnp.dot(
                tv[plan_s[ORDER, p]], hid[plan_s[TAKE, p]], preferred_element_type=f32
            )
            prods[p] = total.astype(bf16)
        return total

    lax.fori_loop(0, TILE_CAP // UNROLL, forward_step, jnp.zeros((BLK, F), f32))
    for b in range(BR):
        has = plan_s[HAS, b].astype(f32)
        part[b % SUB, b // SUB] = (prods[plan_s[LAST, b]].astype(f32) * has).astype(bf16)

    x = col // 2
    yl = col % 2

    def spot(dx, dy):
        return ((x + dx) % 4) * 2 + (yl + dy) % 2

    c_up, c_down, c_across = spot(1, 0), spot(3, 0), spot(0, 1)

    def both(q, dx):
        return part.at[q, pl.ds(((x + dx) % 4) * 2, 2)]

    def add_up(src, dst, q, index):
        return start_remote(
            pending, src, dst.at[q], r_send.at[index, q], r_recv.at[index, q], col=c_up
        )

    def add_down(src, dst, q, index):
        return start_remote(
            pending, src, dst.at[q], r_send.at[index, q], r_recv.at[index, q], col=c_down
        )

    far_in = {}
    from_below = {}
    from_above = {}
    far_in[0] = add_up(both(0, 2), x_far, 0, 0)
    far_in[2] = add_down(both(2, 2), x_far, 2, 0)
    far_in[1] = add_up(both(1, 2), x_far, 1, 0)
    far_in[3] = add_down(both(3, 2), x_far, 3, 0)
    from_below[2] = add_up(both(2, 1), x_below, 2, 1)
    from_above[0] = add_down(both(0, 3), x_above, 0, 2)

    def joined(q, dx):
        far_in[q].wait_recv()
        x_sum[q] = (both(q, dx)[...].astype(f32) + x_far[q].astype(f32)).astype(bf16)
        return x_sum.at[q]

    from_below[0] = add_up(joined(0, 1), x_below, 0, 1)
    from_above[2] = add_down(joined(2, 3), x_above, 2, 2)
    from_below[3] = add_up(both(3, 1), x_below, 3, 1)
    from_above[1] = add_down(both(1, 3), x_above, 1, 2)
    from_below[1] = add_up(joined(1, 1), x_below, 1, 1)
    from_above[3] = add_down(joined(3, 3), x_above, 3, 2)

    y_in = {}
    gathers = {}

    def gather(dx, dy, q, way):
        to, rx, ry = {
            "up": (c_up, (dx + 3) % 4, dy),
            "down": (c_down, (dx + 1) % 4, dy),
            "across": (c_across, dx, 1 - dy),
        }[way]
        piece = grad_t.at[spot(dx, dy) * SUB + q]
        index = rx * 2 + ry
        gathers[rx, ry, q] = start_remote(
            pending, piece, piece, g_send.at[index, q], g_recv.at[index, q], col=to
        )

    def here(dx, dy, q):
        gathers.pop((dx, dy, q)).wait_recv()

    def across_sum(q):
        from_below[q].wait_recv()
        from_above[q].wait_recv()

        def side(dy):
            y = (yl + dy) % 2
            return (
                part[q, spot(0, dy)].astype(f32)
                + x_below[q, y].astype(f32)
                + x_above[q, y].astype(f32)
            )

        y_sum[q] = side(1).astype(bf16)
        y_in[q] = start_remote(
            pending, y_sum.at[q], y_got.at[q], r_send.at[3, q], r_recv.at[3, q], col=c_across
        )
        mine[q] = side(0)

    def activate(q):
        y_in[q].wait_recv()
        pre = mine[q] + y_got[q].astype(f32)
        sig = jax.nn.sigmoid(pre)
        span = pl.ds(q * BLK, BLK)
        act[span] = (pre * sig).astype(bf16)
        grad = cot[span].astype(f32) * sig * (1.0 + pre * (1.0 - sig))
        grad_t[col * SUB + q] = grad.T.astype(bf16)
        for way in ("across", "up", "down") if q % 2 == 0 else ("up", "down", "across"):
            gather(0, 0, q, way)

    across_sum(0)
    across_sum(2)
    activate(0)
    activate(2)
    across_sum(1)
    across_sum(3)
    here(0, 1, 0)
    gather(0, 1, 0, "up")
    gather(0, 1, 0, "down")
    here(0, 1, 2)
    gather(0, 1, 2, "down")
    gather(0, 1, 2, "up")
    activate(1)
    activate(3)
    here(3, 0, 0)
    gather(3, 0, 0, "up")
    here(1, 0, 2)
    gather(1, 0, 2, "down")
    here(3, 1, 0)
    gather(3, 1, 0, "up")
    here(1, 1, 2)
    gather(1, 1, 2, "down")
    here(3, 0, 1)
    gather(3, 0, 1, "up")
    gather(3, 0, 1, "across")
    here(1, 0, 3)
    gather(1, 0, 3, "down")
    gather(1, 0, 3, "across")
    here(3, 0, 3)
    gather(3, 0, 3, "across")
    here(1, 0, 1)
    gather(1, 0, 1, "across")
    here(2, 0, 1)
    gather(2, 0, 1, "across")
    here(2, 0, 3)
    gather(2, 0, 3, "across")
    for key in list(gathers):
        here(*key)

    def backward_step(i, total):
        for t in range(UNROLL):
            p = i * UNROLL + t
            keep = plan_s[5 + KEEP, p].astype(f32)
            total = total * keep + jnp.dot(
                grad_t[plan_s[5 + TAKE, p]], tv[plan_s[5 + ORDER, p]], preferred_element_type=f32
            )
            prods[p] = total.astype(bf16)
        return total

    lax.fori_loop(0, TILE_CAP // UNROLL, backward_step, jnp.zeros((F, BLK), f32))

    chips = [(0, 1), (0, 2), (0, 3), (1, 0), (1, 1), (1, 2), (1, 3), (0, 0)]
    pairs = {}

    def panel_step(i, carry):
        for t in range(8):
            b = i * 8 + t
            has = plan_s[5 + HAS, b].astype(f32)
            block = (prods[plan_s[5 + LAST, b]].astype(f32) * has).astype(bf16)
            back[b] = block
            out = jnp.dot(w, block, preferred_element_type=f32)
            span = pl.ds(pl.multiple_of(b * BLK, BLK), BLK)
            slabs[:, :, span] = out.reshape(NROW, PER, BLK).astype(bf16)
        return carry

    def start_pairs(h, items):
        for dy, dz in items:
            k = chips.index((dy, dz))
            pairs[dy, dz, h] = start_remote(
                pending,
                half(slabs.at[at(dy, dz, other)], h),
                pbuf.at[h, k],
                p_send.at[h, k],
                p_recv.at[h, k],
                row=partner,
            )

    lax.fori_loop(0, BC // 16, panel_step, 0)
    start_pairs(0, [(0, 2), (1, 2), (0, 1), (1, 1), (0, 3), (1, 3), (1, 0), (0, 0)])
    lax.fori_loop(BC // 16, BC // 8, panel_step, 0)
    start_pairs(1, [(1, 2), (1, 1), (1, 3), (1, 0), (0, 2), (0, 1), (0, 3), (0, 0)])

    def pair_sum(dy, dz, h):
        pairs[dy, dz, h].wait_recv()
        k = chips.index((dy, dz))
        own = slabs[at(dy, dz, core), :, h * HALF : (h + 1) * HALF]
        return own.astype(f32) + pbuf[h, k].astype(f32)

    def pass_sum(value, h, k, to):
        sbuf[h, k] = value.astype(bf16)
        return start_remote(
            pending, sbuf.at[h, k], rbuf.at[h, k], s_send.at[h, k], s_recv.at[h, k], row=to
        )

    sums = {}
    for dz in (2, 1, 3):
        for dy in (1, 0):
            k = chips.index((dy, dz))
            sums[dy, dz, 0] = pass_sum(pair_sum(dy, dz, 0), 0, k, at(0, dz, core))
    for dz in (2, 1, 3, 0):
        k = chips.index((1, dz))
        sums[1, dz, 1] = pass_sum(pair_sum(1, dz, 1), 1, k, across)

    def weight_step(i, total):
        for t in range(8):
            b = i * 8 + t
            total = total + lax.dot_general(
                columns(b * BLK, BLK), back[b], (((1,), (1,)), ((), ())), preferred_element_type=f32
            )
        return total

    gw_part = lax.fori_loop(0, BC // 8, weight_step, jnp.zeros((F, F), f32))
    for r in range(NROW):
        gwbuf[r % 2, r // 2] = gw_part[r * PER : (r + 1) * PER]
    gw_pair = start_remote(
        pending, gwbuf.at[other], gwpair, w_send.at[7], w_recv.at[7], row=partner
    )

    for dz in (2, 1, 3):
        k = chips.index((0, dz))
        value = pair_sum(0, dz, 1)
        sums[1, dz, 1].wait_recv()
        value = value + rbuf[1, chips.index((1, dz))].astype(f32)
        sums[0, dz, 1] = pass_sum(value, 1, k, at(0, dz, core))

    value = pair_sum(1, 0, 0)
    for dz in (1, 2, 3):
        sums[1, dz, 0].wait_recv()
        value = value + rbuf[0, chips.index((1, dz))].astype(f32)
    sums[1, 0, 0] = pass_sum(value, 0, chips.index((1, 0)), across)

    gw_pair.wait_recv()
    gwsum[...] = gwbuf[core] + gwpair[...]
    shares = []
    for k, (dy, dz) in enumerate(chips[:7]):
        chip = ((yh + dy) % 2) * 4 + (z + dz) % 4
        shares.append(
            start_remote(
                pending,
                gwsum.at[chip],
                gwrow.at[k],
                w_send.at[k],
                w_recv.at[k],
                row=at(dy, dz, core),
            )
        )

    total = pair_sum(0, 0, 1)
    sums[1, 0, 1].wait_recv()
    total = total + rbuf[1, chips.index((1, 0))].astype(f32)
    for dz in (1, 2, 3):
        sums[0, dz, 1].wait_recv()
        total = total + rbuf[1, chips.index((0, dz))].astype(f32)
    gf[:, HALF:] = total.astype(bf16)

    gw_sum = gwsum[me // 2]
    for k in range(7):
        shares[k].wait_recv()
        gw_sum = gw_sum + gwrow[k]
    gwmine[...] = gw_sum
    spreads = []
    for k in range(1, NCOL):
        spreads.append(
            start_remote(
                pending, gwmine, gwcol.at[k], c_send.at[k], c_recv.at[k], col=cpeers[k - 1]
            )
        )

    total = pair_sum(0, 0, 0)
    for dy, dz in ((0, 1), (0, 2), (0, 3), (1, 0)):
        sums[dy, dz, 0].wait_recv()
        total = total + rbuf[0, chips.index((dy, dz))].astype(f32)
    gf[:, :HALF] = total.astype(bf16)

    for k in range(1, NCOL):
        spreads[k - 1].wait_recv()
        gw_sum = gw_sum + gwcol[k]
    gw[...] = gw_sum
    for copy in pending:
        copy.wait_send()


def dma(*shape):
    return pltpu.SemaphoreType.DMA(shape)


def on_device(features, weight, tiles, tile_rows, tile_cols, tile_count, cotangent):
    sds = jax.ShapeDtypeStruct
    activated, grad_weight, gf_t = pl.pallas_call(
        layer_kernel,
        out_shape=(sds((CHUNK, F), bf16), sds((PER, F), f32), sds((PER, PANEL), bf16)),
        in_specs=[any_spec()] * 7,
        out_specs=(vmem_spec(), vmem_spec(), vmem_spec()),
        scratch_shapes=[
            pltpu.VMEM((F, F), bf16),
            pltpu.VMEM((1, TILE_CAP), i32),
            pltpu.VMEM((1, TILE_CAP), i32),
            pltpu.VMEM((1, 1), i32),
            pltpu.VMEM((CHUNK, F), bf16),
            pltpu.VMEM((TILE_CAP, BLK, BLK), bf16),
            pltpu.VMEM((NROW, PER, PANEL), bf16),
            pltpu.VMEM((BC, BLK, F), bf16),
            pltpu.VMEM((TILE_CAP, BLK, BLK), bf16),
            pltpu.VMEM((SUB, NCOL, BLK, F), bf16),
            pltpu.VMEM((SUB, 2, BLK, F), bf16),
            pltpu.VMEM((SUB, 2, BLK, F), bf16),
            pltpu.VMEM((SUB, 2, BLK, F), bf16),
            pltpu.VMEM((SUB, 2, BLK, F), bf16),
            pltpu.VMEM((SUB, BLK, F), bf16),
            pltpu.VMEM((SUB, BLK, F), bf16),
            pltpu.VMEM((SUB, BLK, F), f32),
            pltpu.VMEM((BR, F, BLK), bf16),
            pltpu.VMEM((BC, F, BLK), bf16),
            pltpu.VMEM((NROW, PER, PANEL), bf16),
            pltpu.VMEM((2, 8, PER, HALF), bf16),
            pltpu.VMEM((2, 7, PER, HALF), bf16),
            pltpu.VMEM((2, 7, PER, HALF), bf16),
            pltpu.VMEM((2, 8, PER, F), f32),
            pltpu.VMEM((8, PER, F), f32),
            pltpu.VMEM((8, PER, F), f32),
            pltpu.VMEM((7, PER, F), f32),
            pltpu.VMEM((PER, F), f32),
            pltpu.VMEM((NCOL, PER, F), f32),
            pltpu.VMEM((16, TILE_CAP), i32),
            pltpu.SMEM((16, TILE_CAP), i32),
            dma(8), dma(15), dma(15), dma(14), dma(14),
            dma(4, SUB), dma(4, SUB), dma(NCOL, SUB), dma(NCOL, SUB),
            dma(2, 8), dma(2, 8), dma(2, 7), dma(2, 7), dma(8), dma(8),
            dma(NCOL), dma(NCOL),
        ],
        compiler_params=pltpu.CompilerParams(
            collective_id=0, has_side_effects=True, vmem_limit_bytes=60 * MIB
        ),
        cost_estimate=pl.CostEstimate(
            flops=4 * TILE_CAP * BLK**3, bytes_accessed=11 * MIB, transcendentals=CHUNK * F
        ),
        name="graph_layer",
    )(features.T, weight, tiles, tile_rows[0], tile_cols[0], tile_count, cotangent)
    return (activated, grad_weight, gf_t.T)


def solution(mesh):
    return jax.shard_map(
        on_device,
        mesh=mesh,
        in_specs=(
            P("col", "row"),
            P(),
            P("row", "col", None, None, None),
            P("row", "col", None),
            P("row", "col", None),
            P("row", "col"),
            P(("row", "col"), None),
        ),
        out_specs=(P(("row", "col"), None), P("row", None), P("col", "row")),
        check_vma=False,
    )
```

time: 90.7 us -> 85.1 us (0.938)
  Pallas kernels: 83.2 us -> 79.1 us
  local copies, waits for them, and re-layouts: 5.82 us -> 4.41 us
    pallas_call x1, Pallas kernels: 83.2 us -> 79.1 us  [on_device(): pl.pallas_call(layer_kernel, out_shape=(sds((CHUNK, F), bf16), sds((PER,...]
    unnamed x13 -> x3, local copies, waits for them, and re-layouts: 5.82 us -> 4.41 us
where the time goes in v3:
time: 85.1 us; the launch traced here: 84.8 us
  Pallas kernels  79.1 us (93%)
  local copies, waits for them, and re-layouts  4.41 us (5%)
  between operations  1.29 us (2%)
    pallas_call x1, Pallas kernels, on_device(): pl.pallas_call(layer_kernel, out_shape=(sds((CHUNK, F), bf16), sds((PER,...  79.1 us
    unnamed x3, local copies, waits for them, and re-layouts  4.41 us

profile of v3, /device:TPU:0, one launch (start us, length us, event | category | flops | bytes accessed | tf_op | source)
XLA Modules:
  0.0 84.8 jit_solution(7849924217115237500)
XLA Ops:
  1.3 79.1 %graph_layer.1 = (bf16[512,128]{1,0:T(8,128)(2,1)}, f32[8,128]{1,0:T(8,128)}, bf16[8,8192]{1,0:T(8,128)(2,1)}) custom-call(bf16[8,8192]{1,0:T(8,128)(2,1)} %bitcast.4, bf16[128,128]{1,0:T(8,128)(2,1)} %weight_in.1, bf16[1,1,256,128,128]{4,3,2,1,0:T(8,128)(2,1)} %tiles.1, s32[1,256]{1,0:T(1,128)} %bitcast.6, s32[1,256]{1,0:T(1,128)} %bitcast.7, ...), custom_call_target="tpu_custom_call" | custom-call | flops 2147483648 | bytes 11534336 | tf_op jit(solution)/shard_map/graph_layer/pallas_call | solution.py:517
  80.4 1.6 %copy.14 = bf16[512,128]{1,0:T(8,128)(2,1)} copy(bf16[512,128]{1,0:T(8,128)(2,1)} %get-tuple-element.12) | data formatting | bytes 262144
  82.0 1.3 %copy.15 = f32[8,128]{1,0:T(8,128)} copy(f32[8,128]{1,0:T(8,128)} %get-tuple-element.13) | data formatting | bytes 8192
  83.2 1.6 %copy.16 = bf16[8192,8]{0,1:T(8,128)(2,1)} copy(bf16[8192,8]{0,1:T(8,128)(2,1)} %bitcast.5) | data formatting | bytes 262144

commit v4 on v3

--- a/solution.py
+++ b/solution.py
@@ -24,6 +24,12 @@
 f32 = jnp.float32
 bf16 = jnp.bfloat16
 i32 = jnp.int32
+
+NSUB = 4
+WIDE = SUB // NSUB
+SUM_PATH = ("yx", "xy", "yx", "xy")
+GATHER_PATH = ("xy", "yx", "xy", "yx")
+SCHEDULE = "f0 f1 f2 f3 s0 s1 s2 s3 e0 e1 e2 e3 g0 g1 g2 g3"
 
 ORDER, TAKE, KEEP, LAST, HAS = range(5)
 
@@ -78,7 +84,7 @@
     feat_in, weight_in, tiles, rows_in, cols_in, count_in, cot_in,
     act, gw, gf,
     weight, rows_v, cols_v, count_v, cot,
-    tv, feat, hid, prods, part, x_far, x_sum, x_below, x_above, y_sum, y_got, mine, grad_t,
+    tv, feat, hid, prods, part, x_sum, x_in, y_in, d_in, grad_t,
     back, slabs, pbuf, sbuf, rbuf, gwbuf, gwpair, gwsum, gwrow, gwmine, gwcol, plan_v, plan_s,
     l_sem, a_send, a_recv, f_send, f_recv, r_send, r_recv, g_send, g_recv,
     p_send, p_recv, s_send, s_recv, w_send, w_recv, c_send, c_recv,
@@ -234,7 +240,9 @@
     lax.fori_loop(0, TILE_CAP // UNROLL, forward_step, jnp.zeros((BLK, F), f32))
     for b in range(BR):
         has = plan_s[HAS, b].astype(f32)
-        part[b % SUB, b // SUB] = (prods[plan_s[LAST, b]].astype(f32) * has).astype(bf16)
+        sub, place = b % SUB // WIDE, b % SUB % WIDE * BLK
+        block = (prods[plan_s[LAST, b]].astype(f32) * has).astype(bf16)
+        part[sub, b // SUB, place : place + BLK] = block
 
     x = col // 2
     yl = col % 2
@@ -242,126 +250,112 @@
     def spot(dx, dy):
         return ((x + dx) % 4) * 2 + (yl + dy) % 2
 
-    c_up, c_down, c_across = spot(1, 0), spot(3, 0), spot(0, 1)
-
     def both(q, dx):
         return part.at[q, pl.ds(((x + dx) % 4) * 2, 2)]
 
-    def add_up(src, dst, q, index):
+    def add_to(src, dst, q, index, to):
         return start_remote(
-            pending, src, dst.at[q], r_send.at[index, q], r_recv.at[index, q], col=c_up
+            pending, src, dst, r_send.at[index, q], r_recv.at[index, q], col=to
         )
 
-    def add_down(src, dst, q, index):
-        return start_remote(
-            pending, src, dst.at[q], r_send.at[index, q], r_recv.at[index, q], col=c_down
-        )
-
-    far_in = {}
-    from_below = {}
-    from_above = {}
-    far_in[0] = add_up(both(0, 2), x_far, 0, 0)
-    far_in[2] = add_down(both(2, 2), x_far, 2, 0)
-    far_in[1] = add_up(both(1, 2), x_far, 1, 0)
-    far_in[3] = add_down(both(3, 2), x_far, 3, 0)
-    from_below[2] = add_up(both(2, 1), x_below, 2, 1)
-    from_above[0] = add_down(both(0, 3), x_above, 0, 2)
-
-    def joined(q, dx):
-        far_in[q].wait_recv()
-        x_sum[q] = (both(q, dx)[...].astype(f32) + x_far[q].astype(f32)).astype(bf16)
-        return x_sum.at[q]
-
-    from_below[0] = add_up(joined(0, 1), x_below, 0, 1)
-    from_above[2] = add_down(joined(2, 3), x_above, 2, 2)
-    from_below[3] = add_up(both(3, 1), x_below, 3, 1)
-    from_above[1] = add_down(both(1, 3), x_above, 1, 2)
-    from_below[1] = add_up(joined(1, 1), x_below, 1, 1)
-    from_above[3] = add_down(joined(3, 3), x_above, 3, 2)
-
-    y_in = {}
+    x_got = {}
+    y_got = {}
+    every = [(2, 1), (2, 0), (1, 1), (3, 1), (1, 0), (3, 0), (0, 1)]
+    def first(q):
+        if SUM_PATH[q] == "yx":
+            for dx in (2, 1, 3, 0):
+                src = part.at[q, spot(dx, 1)]
+                y_got[q, dx] = add_to(src, y_in.at[q, dx], q, 4 + dx, spot(0, 1))
+        elif SUM_PATH[q] == "xy":
+            for dx in (2, 1, 3):
+                x_got[q, dx] = add_to(both(q, dx), x_in.at[q, dx], q, dx, spot(dx, 0))
+        else:
+            for k, (dx, dy) in enumerate(every):
+                src = part.at[q, spot(dx, dy)]
+                x_got[q, k] = add_to(src, d_in.at[q, k], q, 8 + k, spot(dx, dy))
+
+    def second(q):
+        if SUM_PATH[q] == "yx":
+            for dx in (2, 1, 3):
+                y_got[q, dx].wait_recv()
+                x_sum[q, dx] = (
+                    part[q, spot(dx, 0)].astype(f32) + y_in[q, dx].astype(f32)
+                ).astype(bf16)
+                x_got[q, dx] = add_to(x_sum.at[q, dx], x_in.at[q, dx, 0], q, dx, spot(dx, 0))
+        elif SUM_PATH[q] == "xy":
+            side = part[q, spot(0, 1)].astype(f32)
+            for dx in (2, 1, 3):
+                x_got[q, dx].wait_recv()
+                side = side + x_in[q, dx, (yl + 1) % 2].astype(f32)
+            x_sum[q, 0] = side.astype(bf16)
+            y_got[q, 0] = add_to(x_sum.at[q, 0], y_in.at[q, 0], q, 4, spot(0, 1))
+
+    def summed(q):
+        pre = part[q, col].astype(f32)
+        if SUM_PATH[q] == "direct":
+            for k in range(NCOL - 1):
+                x_got[q, k].wait_recv()
+                pre = pre + d_in[q, k].astype(f32)
+            return pre
+        for dx in (2, 1, 3):
+            if SUM_PATH[q] == "yx":
+                x_got[q, dx].wait_recv()
+                pre = pre + x_in[q, dx, 0].astype(f32)
+            else:
+                pre = pre + x_in[q, dx, yl].astype(f32)
+        y_got[q, 0].wait_recv()
+        return pre + y_in[q, 0].astype(f32)
+
     gathers = {}
 
-    def gather(dx, dy, q, way):
-        to, rx, ry = {
-            "up": (c_up, (dx + 3) % 4, dy),
-            "down": (c_down, (dx + 1) % 4, dy),
-            "across": (c_across, dx, 1 - dy),
-        }[way]
-        piece = grad_t.at[spot(dx, dy) * SUB + q]
+    def gather(dx, dy, q, tx, ty):
+        piece = grad_t.at[pl.ds(spot(dx, dy) * SUB + q * WIDE, WIDE)]
+        rx, ry = (dx - tx) % 4, (dy - ty) % 2
         index = rx * 2 + ry
         gathers[rx, ry, q] = start_remote(
-            pending, piece, piece, g_send.at[index, q], g_recv.at[index, q], col=to
+            pending, piece, piece, g_send.at[index, q], g_recv.at[index, q], col=spot(tx, ty)
         )
 
     def here(dx, dy, q):
         gathers.pop((dx, dy, q)).wait_recv()
 
-    def across_sum(q):
-        from_below[q].wait_recv()
-        from_above[q].wait_recv()
-
-        def side(dy):
-            y = (yl + dy) % 2
-            return (
-                part[q, spot(0, dy)].astype(f32)
-                + x_below[q, y].astype(f32)
-                + x_above[q, y].astype(f32)
-            )
-
-        y_sum[q] = side(1).astype(bf16)
-        y_in[q] = start_remote(
-            pending, y_sum.at[q], y_got.at[q], r_send.at[3, q], r_recv.at[3, q], col=c_across
-        )
-        mine[q] = side(0)
-
-    def activate(q):
-        y_in[q].wait_recv()
-        pre = mine[q] + y_got[q].astype(f32)
+    def finish(q):
+        pre = summed(q)
         sig = jax.nn.sigmoid(pre)
-        span = pl.ds(q * BLK, BLK)
+        span = pl.ds(q * WIDE * BLK, WIDE * BLK)
+        grad = cot[span].astype(f32) * sig * (1.0 + pre * (1.0 - sig))
+        for i in range(WIDE):
+            block = grad[i * BLK : (i + 1) * BLK].T
+            grad_t[col * SUB + q * WIDE + i] = block.astype(bf16)
+        if GATHER_PATH[q] == "yx":
+            ways = [(0, 1), (2, 0), (1, 0), (3, 0)]
+        elif GATHER_PATH[q] == "xy":
+            ways = [(2, 0), (1, 0), (3, 0), (0, 1)]
+        else:
+            ways = every
+        for tx, ty in ways:
+            gather(0, 0, q, tx, ty)
         act[span] = (pre * sig).astype(bf16)
-        grad = cot[span].astype(f32) * sig * (1.0 + pre * (1.0 - sig))
-        grad_t[col * SUB + q] = grad.T.astype(bf16)
-        for way in ("across", "up", "down") if q % 2 == 0 else ("up", "down", "across"):
-            gather(0, 0, q, way)
-
-    across_sum(0)
-    across_sum(2)
-    activate(0)
-    activate(2)
-    across_sum(1)
-    across_sum(3)
-    here(0, 1, 0)
-    gather(0, 1, 0, "up")
-    gather(0, 1, 0, "down")
-    here(0, 1, 2)
-    gather(0, 1, 2, "down")
-    gather(0, 1, 2, "up")
-    activate(1)
-    activate(3)
-    here(3, 0, 0)
-    gather(3, 0, 0, "up")
-    here(1, 0, 2)
-    gather(1, 0, 2, "down")
-    here(3, 1, 0)
-    gather(3, 1, 0, "up")
-    here(1, 1, 2)
-    gather(1, 1, 2, "down")
-    here(3, 0, 1)
-    gather(3, 0, 1, "up")
-    gather(3, 0, 1, "across")
-    here(1, 0, 3)
-    gather(1, 0, 3, "down")
-    gather(1, 0, 3, "across")
-    here(3, 0, 3)
-    gather(3, 0, 3, "across")
-    here(1, 0, 1)
-    gather(1, 0, 1, "across")
-    here(2, 0, 1)
-    gather(2, 0, 1, "across")
-    here(2, 0, 3)
-    gather(2, 0, 3, "across")
+
+    def spread(q):
+        if GATHER_PATH[q] == "yx":
+            here(0, 1, q)
+            for tx in (2, 1, 3):
+                gather(0, 1, q, tx, 0)
+        elif GATHER_PATH[q] == "xy":
+            for dx in (3, 1, 2):
+                here(dx, 0, q)
+                gather(dx, 0, q, 0, 1)
+
+    def drain(q):
+        got = [v for d in (x_got, y_got) for key, v in d.items() if key[0] == q]
+        for copy in got:
+            copy.wait_send()
+            pending[:] = [other_copy for other_copy in pending if other_copy is not copy]
+
+    steps = {"f": first, "s": second, "e": finish, "g": spread, "d": drain}
+    for step in SCHEDULE.split():
+        steps[step[0]](int(step[1]))
     for key in list(gathers):
         here(*key)
 
@@ -508,15 +502,33 @@
         copy.wait_send()
 
 
+def write_kernel(act, gw, gf, act_out, gw_out, gf_out, act_v, gw_v, gf_v, sem):
+    def copies(ends, base):
+        return [
+            pltpu.make_async_copy(src, dst, sem.at[base + i]) for i, (src, dst) in enumerate(ends)
+        ]
+
+    reads = copies([(gf, gf_v), (act, act_v), (gw, gw_v)], 0)
+    writes = copies([(gf_v, gf_out), (act_v, act_out), (gw_v, gw_out)], 3)
+    for copy in reads:
+        copy.start()
+    for read, write in zip(reads, writes):
+        read.wait()
+        write.start()
+    for copy in writes:
+        copy.wait()
+
+
 def dma(*shape):
     return pltpu.SemaphoreType.DMA(shape)
 
 
 def on_device(features, weight, tiles, tile_rows, tile_cols, tile_count, cotangent):
     sds = jax.ShapeDtypeStruct
-    activated, grad_weight, gf_t = pl.pallas_call(
+    shapes = (sds((CHUNK, F), bf16), sds((PER, F), f32), sds((PER, PANEL), bf16))
+    outs = pl.pallas_call(
         layer_kernel,
-        out_shape=(sds((CHUNK, F), bf16), sds((PER, F), f32), sds((PER, PANEL), bf16)),
+        out_shape=shapes,
         in_specs=[any_spec()] * 7,
         out_specs=(vmem_spec(), vmem_spec(), vmem_spec()),
         scratch_shapes=[
@@ -529,14 +541,11 @@
             pltpu.VMEM((NROW, PER, PANEL), bf16),
             pltpu.VMEM((BC, BLK, F), bf16),
             pltpu.VMEM((TILE_CAP, BLK, BLK), bf16),
-            pltpu.VMEM((SUB, NCOL, BLK, F), bf16),
-            pltpu.VMEM((SUB, 2, BLK, F), bf16),
-            pltpu.VMEM((SUB, 2, BLK, F), bf16),
-            pltpu.VMEM((SUB, 2, BLK, F), bf16),
-            pltpu.VMEM((SUB, 2, BLK, F), bf16),
-            pltpu.VMEM((SUB, BLK, F), bf16),
-            pltpu.VMEM((SUB, BLK, F), bf16),
-            pltpu.VMEM((SUB, BLK, F), f32),
+            pltpu.VMEM((NSUB, NCOL, WIDE * BLK, F), bf16),
+            pltpu.VMEM((NSUB, 4, WIDE * BLK, F), bf16),
+            pltpu.VMEM((NSUB, 4, 2, WIDE * BLK, F), bf16),
+            pltpu.VMEM((NSUB, 4, WIDE * BLK, F), bf16),
+            pltpu.VMEM((NSUB, NCOL - 1, WIDE * BLK, F), bf16),
             pltpu.VMEM((BR, F, BLK), bf16),
             pltpu.VMEM((BC, F, BLK), bf16),
             pltpu.VMEM((NROW, PER, PANEL), bf16),
@@ -552,7 +561,7 @@
             pltpu.VMEM((16, TILE_CAP), i32),
             pltpu.SMEM((16, TILE_CAP), i32),
             dma(8), dma(15), dma(15), dma(14), dma(14),
-            dma(4, SUB), dma(4, SUB), dma(NCOL, SUB), dma(NCOL, SUB),
+            dma(16, NSUB), dma(16, NSUB), dma(NCOL, NSUB), dma(NCOL, NSUB),
             dma(2, 8), dma(2, 8), dma(2, 7), dma(2, 7), dma(8), dma(8),
             dma(NCOL), dma(NCOL),
         ],
@@ -564,6 +573,15 @@
         ),
         name="graph_layer",
     )(features.T, weight, tiles, tile_rows[0], tile_cols[0], tile_count, cotangent)
+    activated, grad_weight, gf_t = pl.pallas_call(
+        write_kernel,
+        out_shape=shapes,
+        in_specs=[any_spec()] * 3,
+        out_specs=(any_spec(),) * 3,
+        scratch_shapes=[pltpu.VMEM(x.shape, x.dtype) for x in shapes] + [dma(6)],
+        compiler_params=pltpu.CompilerParams(vmem_limit_bytes=60 * MIB),
+        name="write_results",
+    )(*outs)
     return (activated, grad_weight, gf_t.T)
 
 

time: 85.1 us -> 77.7 us (0.913)
  local copies, waits for them, and re-layouts: 4.41 us -> 0 us
  Pallas kernels: 79.1 us -> 76.2 us
    unnamed x3 -> x0, local copies, waits for them, and re-layouts: 4.41 us -> none
    pallas_call x1 -> x2, Pallas kernels: 79.1 us -> 76.2 us  [the longest x1 74.6 us: on_device(): pl.pallas_call(layer_kernel, out_shape=shapes, in_specs=[any_spec()] * 7,...]
where the time goes in v4:
time: 77.7 us; the launch traced here: 77.5 us
  Pallas kernels  76.2 us (98%)
  between operations  1.29 us (2%)
    pallas_call x1, Pallas kernels, on_device(): pl.pallas_call(layer_kernel, out_shape=shapes, in_specs=[any_spec()] * 7,...  74.6 us
    pallas_call x1, Pallas kernels, on_device(): pl.pallas_call(write_kernel, out_shape=shapes, in_specs=[any_spec()] * 3,...  1.68 us

profile of v4, /device:TPU:0, one launch (start us, length us, event | category | flops | bytes accessed | tf_op | source)
XLA Modules:
  0.0 77.5 jit_solution(84167879206305350)
XLA Ops:
  1.3 74.6 %graph_layer.1 = (bf16[512,128]{1,0:T(8,128)(2,1)}, f32[8,128]{1,0:T(8,128)}, bf16[8,8192]{1,0:T(8,128)(2,1)}) custom-call(bf16[8,8192]{1,0:T(8,128)(2,1)} %bitcast.4, bf16[128,128]{1,0:T(8,128)(2,1)} %weight_in.1, bf16[1,1,256,128,128]{4,3,2,1,0:T(8,128)(2,1)} %tiles.1, s32[1,256]{1,0:T(1,128)} %bitcast.5, s32[1,256]{1,0:T(1,128)} %bitcast.6, ...), custom_call_target="tpu_custom_call" | custom-call | flops 2147483648 | bytes 11534336 | tf_op jit(solution)/shard_map/graph_layer/pallas_call | solution.py:529
  75.9 1.7 %write_results.1 = (bf16[512,128]{1,0:T(8,128)(2,1)}, f32[8,128]{1,0:T(8,128)}, bf16[8,8192]{1,0:T(8,128)(2,1)}) custom-call(bf16[512,128]{1,0:T(8,128)(2,1)} %get-tuple-element.9.act, f32[8,128]{1,0:T(8,128)} %get-tuple-element.10.gw, bf16[8,8192]{1,0:T(8,128)(2,1)} %get-tuple-element.11.gf), custom_call_target="tpu_custom_call" | custom-call | tf_op jit(solution)/shard_map/write_results/pallas_call | solution.py:576

commit v5 on v4

--- a/solution.py
+++ b/solution.py
@@ -17,7 +17,7 @@
 CHUNK = 512
 SUB = CHUNK // BLK
 PER = F // NROW
-UNROLL = 32
+UNROLL = 64
 MIB = 1024 * 1024
 MESH = pl.DeviceIdType.MESH
 
@@ -84,7 +84,7 @@
     feat_in, weight_in, tiles, rows_in, cols_in, count_in, cot_in,
     act, gw, gf,
     weight, rows_v, cols_v, count_v, cot,
-    tv, feat, hid, prods, part, x_sum, x_in, y_in, d_in, grad_t,
+    tv, feat, feat_n, hid, prods, part, x_sum, x_in, y_in, d_in, grad_t,
     back, slabs, pbuf, sbuf, rbuf, gwbuf, gwpair, gwsum, gwrow, gwmine, gwcol, plan_v, plan_s,
     l_sem, a_send, a_recv, f_send, f_recv, r_send, r_recv, g_send, g_recv,
     p_send, p_recv, s_send, s_recv, w_send, w_recv, c_send, c_recv,
@@ -100,7 +100,7 @@
         return ((yh + dy) % 2) * 8 + ((z + dz) % 4) * 2 + k
 
     partner = at(0, 0, other)
-    up, down, across = at(0, 1, core), at(0, 3, core), at(1, 0, core)
+    across = at(1, 0, core)
     peers = [partner] + [at(dy, dz, core) for dy in (0, 1) for dz in range(4) if dy + dz]
     cpeers = [(col + k) % NCOL for k in range(1, NCOL)]
 
@@ -128,22 +128,26 @@
     def half(ref, h):
         return ref.at[:, pl.ds(h * HALF, HALF)]
 
-    def send(src, slab, h, index, to):
-        dst = feat.at[slab] if h is None else half(feat.at[slab], h)
-        copy = start_remote(pending, src, dst, a_send.at[index], a_recv.at[index], row=to)
-        return copy
-
-    def pass_on(slab, h, index, to):
-        return send(half(feat.at[slab], h), slab, h, index, to)
-
     got = {}
-    got["d", 0] = send(half(feat_in, 0), me, 0, 0, up)
-    got["u", 1] = send(half(feat_in, 1), me, 1, 3, down)
-    got["y", 0] = send(half(feat_in, 0), me, 0, 4, across)
-    got["y", 1] = send(half(feat_in, 1), me, 1, 5, across)
-    got["d", 1] = send(half(feat_in, 1), me, 1, 1, up)
-    got["u", 0] = send(half(feat_in, 0), me, 0, 2, down)
-    got["c", 2] = send(feat_in, me, None, 6, partner)
+
+    def send(dy, dz, h, ty, tz):
+        piece = half(feat.at[at(dy, dz, core)], h)
+        src = half(feat_in, h) if (dy, dz) == (0, 0) else piece
+        ry, rz = (dy - ty) % 2, (dz - tz) % 4
+        index = h * 8 + ry * 4 + rz
+        got[ry, rz, h] = start_remote(
+            pending, src, piece, a_send.at[index], a_recv.at[index], row=at(ty, tz, core)
+        )
+
+    send(0, 0, 1, 1, 0)
+    for tz in (2, 1, 3):
+        send(0, 0, 0, 0, tz)
+    send(0, 0, 0, 1, 0)
+    for tz in (2, 1, 3):
+        send(0, 0, 1, 0, tz)
+    own_hand = start_remote(
+        pending, feat_in, feat.at[me], f_send.at[0], f_recv.at[0], row=partner
+    )
 
     for copy in small:
         copy.wait()
@@ -155,74 +159,47 @@
     plan_copy = pltpu.make_async_copy(plan_v, plan_s, l_sem.at[2])
     plan_copy.start()
 
-    handed = []
-
-    def hand(slab, h):
+    handed = [own_hand]
+
+    def hand(dy, dz, h):
         index = len(handed)
-        piece = half(feat.at[slab], h)
-        copy = start_remote(pending, piece, piece, f_send.at[index], f_recv.at[index], row=partner)
-        handed.append(copy)
-
-    below, above = at(0, 3, core), at(0, 1, core)
-    far = at(0, 2, core)
-    y_own, y_below, y_above, y_far = (at(1, d, core) for d in (0, 3, 1, 2))
-
-    got["d", 0].wait_recv()
-    got["far", 0] = pass_on(below, 0, 7, up)
-    hand(below, 0)
-    got["u", 1].wait_recv()
-    got["far", 1] = pass_on(above, 1, 8, down)
-    hand(above, 1)
-    got["y", 0].wait_recv()
-    got["yd", 0] = pass_on(y_own, 0, 9, up)
-    got["y", 1].wait_recv()
-    got["yu", 1] = pass_on(y_own, 1, 12, down)
-    got["yd", 1] = pass_on(y_own, 1, 10, up)
-    got["yu", 0] = pass_on(y_own, 0, 11, down)
-    hand(y_own, 0)
-    hand(y_own, 1)
-    got["d", 1].wait_recv()
-    hand(below, 1)
-    got["u", 0].wait_recv()
-    hand(above, 0)
-    got["far", 0].wait_recv()
-    got["yfar", 0] = pass_on(far, 0, 13, across)
-    hand(far, 0)
-    got["far", 1].wait_recv()
-    got["yfar", 1] = pass_on(far, 1, 14, across)
-    hand(far, 1)
-    got["yd", 0].wait_recv()
-    hand(y_below, 0)
-    got["yu", 1].wait_recv()
-    hand(y_above, 1)
-    got["yd", 1].wait_recv()
-    hand(y_below, 1)
-    got["yu", 0].wait_recv()
-    hand(y_above, 0)
-    got["yfar", 0].wait_recv()
-    hand(y_far, 0)
-    got["yfar", 1].wait_recv()
-    hand(y_far, 1)
-    got["c", 2].wait_recv()
+        piece = half(feat.at[at(dy, dz, core)], h)
+        handed.append(
+            start_remote(
+                pending, piece, piece, f_send.at[index], f_recv.at[index], row=partner
+            )
+        )
+
+    got[1, 0, 1].wait_recv()
+    for tz in (2, 1, 3):
+        send(1, 0, 1, 0, tz)
+    hand(1, 0, 1)
+    for dz in (1, 3, 2):
+        got[0, dz, 0].wait_recv()
+        send(0, dz, 0, 1, 0)
+        hand(0, dz, 0)
+    for dy, dz, h in (
+        (1, 0, 0), (0, 1, 1), (0, 3, 1), (0, 2, 1), (1, 1, 0), (1, 3, 0), (1, 2, 0),
+        (1, 1, 1), (1, 3, 1), (1, 2, 1),
+    ):
+        got[dy, dz, h].wait_recv()
+        hand(dy, dz, h)
     own_copy.wait()
     for copy in handed:
         copy.wait_recv()
 
-    def columns(start, width):
-        span = pl.ds(pl.multiple_of(start, BLK), width)
-        return feat[:, :, span].astype(f32).reshape(F, width).astype(bf16)
-
     w = weight[...]
 
     def hidden_step(i, carry):
-        for t in range(8):
-            b = i * 8 + t
-            hid[b] = lax.dot_general(
-                columns(b * BLK, BLK), w, (((0,), (0,)), ((), ())), preferred_element_type=f32
-            ).astype(bf16)
+        for t in range(16):
+            b = i * 16 + t
+            span = pl.ds(pl.multiple_of(b * BLK, BLK), BLK)
+            nodes = feat[:, :, span].astype(f32).reshape(F, BLK).T.astype(bf16)
+            feat_n[b] = nodes
+            hid[b] = jnp.dot(nodes, w, preferred_element_type=f32).astype(bf16)
         return carry
 
-    lax.fori_loop(0, BC // 8, hidden_step, 0)
+    lax.fori_loop(0, BC // 16, hidden_step, 0)
 
     plan_copy.wait()
     tile_copy.wait()
@@ -374,16 +351,17 @@
     chips = [(0, 1), (0, 2), (0, 3), (1, 0), (1, 1), (1, 2), (1, 3), (0, 0)]
     pairs = {}
 
-    def panel_step(i, carry):
-        for t in range(8):
-            b = i * 8 + t
+    def panel_step(i, total):
+        for t in range(16):
+            b = i * 16 + t
             has = plan_s[5 + HAS, b].astype(f32)
             block = (prods[plan_s[5 + LAST, b]].astype(f32) * has).astype(bf16)
             back[b] = block
             out = jnp.dot(w, block, preferred_element_type=f32)
             span = pl.ds(pl.multiple_of(b * BLK, BLK), BLK)
             slabs[:, :, span] = out.reshape(NROW, PER, BLK).astype(bf16)
-        return carry
+            total = total + jnp.dot(block, feat_n[b], preferred_element_type=f32)
+        return total
 
     def start_pairs(h, items):
         for dy, dz in items:
@@ -397,10 +375,16 @@
                 row=partner,
             )
 
-    lax.fori_loop(0, BC // 16, panel_step, 0)
+    gw_part = lax.fori_loop(0, BC // 32, panel_step, jnp.zeros((F, F), f32))
     start_pairs(0, [(0, 2), (1, 2), (0, 1), (1, 1), (0, 3), (1, 3), (1, 0), (0, 0)])
-    lax.fori_loop(BC // 16, BC // 8, panel_step, 0)
-    start_pairs(1, [(1, 2), (1, 1), (1, 3), (1, 0), (0, 2), (0, 1), (0, 3), (0, 0)])
+    gw_part = lax.fori_loop(BC // 32, BC // 16, panel_step, gw_part)
+    gw_part = gw_part.T
+    for r in range(NROW):
+        gwbuf[r % 2, r // 2] = gw_part[r * PER : (r + 1) * PER]
+    gw_pair = start_remote(
+        pending, gwbuf.at[other], gwpair, w_send.at[7], w_recv.at[7], row=partner
+    )
+
 
     def pair_sum(dy, dz, h):
         pairs[dy, dz, h].wait_recv()
@@ -414,42 +398,7 @@
             pending, sbuf.at[h, k], rbuf.at[h, k], s_send.at[h, k], s_recv.at[h, k], row=to
         )
 
-    sums = {}
-    for dz in (2, 1, 3):
-        for dy in (1, 0):
-            k = chips.index((dy, dz))
-            sums[dy, dz, 0] = pass_sum(pair_sum(dy, dz, 0), 0, k, at(0, dz, core))
-    for dz in (2, 1, 3, 0):
-        k = chips.index((1, dz))
-        sums[1, dz, 1] = pass_sum(pair_sum(1, dz, 1), 1, k, across)
-
-    def weight_step(i, total):
-        for t in range(8):
-            b = i * 8 + t
-            total = total + lax.dot_general(
-                columns(b * BLK, BLK), back[b], (((1,), (1,)), ((), ())), preferred_element_type=f32
-            )
-        return total
-
-    gw_part = lax.fori_loop(0, BC // 8, weight_step, jnp.zeros((F, F), f32))
-    for r in range(NROW):
-        gwbuf[r % 2, r // 2] = gw_part[r * PER : (r + 1) * PER]
-    gw_pair = start_remote(
-        pending, gwbuf.at[other], gwpair, w_send.at[7], w_recv.at[7], row=partner
-    )
-
-    for dz in (2, 1, 3):
-        k = chips.index((0, dz))
-        value = pair_sum(0, dz, 1)
-        sums[1, dz, 1].wait_recv()
-        value = value + rbuf[1, chips.index((1, dz))].astype(f32)
-        sums[0, dz, 1] = pass_sum(value, 1, k, at(0, dz, core))
-
-    value = pair_sum(1, 0, 0)
-    for dz in (1, 2, 3):
-        sums[1, dz, 0].wait_recv()
-        value = value + rbuf[0, chips.index((1, dz))].astype(f32)
-    sums[1, 0, 0] = pass_sum(value, 0, chips.index((1, 0)), across)
+    start_pairs(1, [(1, 2), (1, 1), (1, 3), (1, 0), (0, 2), (0, 1), (0, 3), (0, 0)])
 
     gw_pair.wait_recv()
     gwsum[...] = gwbuf[core] + gwpair[...]
@@ -467,13 +416,21 @@
             )
         )
 
-    total = pair_sum(0, 0, 1)
-    sums[1, 0, 1].wait_recv()
-    total = total + rbuf[1, chips.index((1, 0))].astype(f32)
-    for dz in (1, 2, 3):
-        sums[0, dz, 1].wait_recv()
-        total = total + rbuf[1, chips.index((0, dz))].astype(f32)
-    gf[:, HALF:] = total.astype(bf16)
+    sums = {}
+    for dz in (2, 1, 3):
+        for dy in (1, 0):
+            k = chips.index((dy, dz))
+            sums[dy, dz, 0] = pass_sum(pair_sum(dy, dz, 0), 0, k, at(0, dz, core))
+    for dz in (2, 1, 3, 0):
+        k = chips.index((1, dz))
+        sums[1, dz, 1] = pass_sum(pair_sum(1, dz, 1), 1, k, across)
+
+    for dz in (2, 1, 3):
+        k = chips.index((0, dz))
+        value = pair_sum(0, dz, 1)
+        sums[1, dz, 1].wait_recv()
+        value = value + rbuf[1, chips.index((1, dz))].astype(f32)
+        sums[0, dz, 1] = pass_sum(value, 1, k, at(0, dz, core))
 
     gw_sum = gwsum[me // 2]
     for k in range(7):
@@ -487,6 +444,20 @@
                 pending, gwmine, gwcol.at[k], c_send.at[k], c_recv.at[k], col=cpeers[k - 1]
             )
         )
+
+    value = pair_sum(1, 0, 0)
+    for dz in (1, 2, 3):
+        sums[1, dz, 0].wait_recv()
+        value = value + rbuf[0, chips.index((1, dz))].astype(f32)
+    sums[1, 0, 0] = pass_sum(value, 0, chips.index((1, 0)), across)
+
+    total = pair_sum(0, 0, 1)
+    sums[1, 0, 1].wait_recv()
+    total = total + rbuf[1, chips.index((1, 0))].astype(f32)
+    for dz in (1, 2, 3):
+        sums[0, dz, 1].wait_recv()
+        total = total + rbuf[1, chips.index((0, dz))].astype(f32)
+    gf[:, HALF:] = total.astype(bf16)
 
     total = pair_sum(0, 0, 0)
     for dy, dz in ((0, 1), (0, 2), (0, 3), (1, 0)):
@@ -539,6 +510,7 @@
             pltpu.VMEM((CHUNK, F), bf16),
             pltpu.VMEM((TILE_CAP, BLK, BLK), bf16),
             pltpu.VMEM((NROW, PER, PANEL), bf16),
+            pltpu.VMEM((BC, BLK, F), bf16),
             pltpu.VMEM((BC, BLK, F), bf16),
             pltpu.VMEM((TILE_CAP, BLK, BLK), bf16),
             pltpu.VMEM((NSUB, NCOL, WIDE * BLK, F), bf16),
@@ -560,7 +532,7 @@
             pltpu.VMEM((NCOL, PER, F), f32),
             pltpu.VMEM((16, TILE_CAP), i32),
             pltpu.SMEM((16, TILE_CAP), i32),
-            dma(8), dma(15), dma(15), dma(14), dma(14),
+            dma(8), dma(16), dma(16), dma(15), dma(15),
             dma(16, NSUB), dma(16, NSUB), dma(NCOL, NSUB), dma(NCOL, NSUB),
             dma(2, 8), dma(2, 8), dma(2, 7), dma(2, 7), dma(8), dma(8),
             dma(NCOL), dma(NCOL),

time: 77.7 us -> 70.4 us (0.906)
  Pallas kernels: 76.2 us -> 68.3 us
    pallas_call x1, Pallas kernels: 74.6 us -> 66.6 us  [on_device(): pl.pallas_call(layer_kernel, out_shape=shapes, in_specs=[any_spec()] * 7,...]
where the time goes in v5:
time: 70.4 us; the launch traced here: 69.6 us
  Pallas kernels  68.3 us (97%)
  between operations  1.29 us (2%)
    pallas_call x1, Pallas kernels, on_device(): pl.pallas_call(layer_kernel, out_shape=shapes, in_specs=[any_spec()] * 7,...  66.6 us
    pallas_call x1, Pallas kernels, on_device(): pl.pallas_call(write_kernel, out_shape=shapes, in_specs=[any_spec()] * 3,...  1.68 us

profile of v5, /device:TPU:0, one launch (start us, length us, event | category | flops | bytes accessed | tf_op | source)
XLA Modules:
  0.0 69.6 jit_solution(15529488597538858701)
XLA Ops:
  1.3 66.6 %graph_layer.1 = (bf16[512,128]{1,0:T(8,128)(2,1)}, f32[8,128]{1,0:T(8,128)}, bf16[8,8192]{1,0:T(8,128)(2,1)}) custom-call(bf16[8,8192]{1,0:T(8,128)(2,1)} %bitcast.4, bf16[128,128]{1,0:T(8,128)(2,1)} %weight_in.1, bf16[1,1,256,128,128]{4,3,2,1,0:T(8,128)(2,1)} %tiles.1, s32[1,256]{1,0:T(1,128)} %bitcast.5, s32[1,256]{1,0:T(1,128)} %bitcast.6, ...), custom_call_target="tpu_custom_call" | custom-call | flops 2147483648 | bytes 11534336 | tf_op jit(solution)/shard_map/graph_layer/pallas_call | solution.py:500
  67.9 1.7 %write_results.1 = (bf16[512,128]{1,0:T(8,128)(2,1)}, f32[8,128]{1,0:T(8,128)}, bf16[8,8192]{1,0:T(8,128)(2,1)}) custom-call(bf16[512,128]{1,0:T(8,128)(2,1)} %get-tuple-element.9.act, f32[8,128]{1,0:T(8,128)} %get-tuple-element.10.gw, bf16[8,8192]{1,0:T(8,128)(2,1)} %get-tuple-element.11.gf), custom_call_target="tpu_custom_call" | custom-call | tf_op jit(solution)/shard_map/write_results/pallas_call | solution.py:548

commit v6 on v5

--- a/solution.py
+++ b/solution.py
@@ -17,7 +17,7 @@
 CHUNK = 512
 SUB = CHUNK // BLK
 PER = F // NROW
-UNROLL = 64
+UNROLL = 128
 MIB = 1024 * 1024
 MESH = pl.DeviceIdType.MESH
 
@@ -36,10 +36,6 @@
 
 def any_spec():
     return pl.BlockSpec(memory_space=pl.ANY)
-
-
-def vmem_spec():
-    return pl.BlockSpec(memory_space=pltpu.VMEM)
 
 
 def start_remote(pending, src, dst, send, recv, **where):
@@ -82,8 +78,8 @@
 
 def layer_kernel(
     feat_in, weight_in, tiles, rows_in, cols_in, count_in, cot_in,
-    act, gw, gf,
-    weight, rows_v, cols_v, count_v, cot,
+    act_out, gw_out, gf_out,
+    act, gw, gf, weight, rows_v, cols_v, count_v, cot,
     tv, feat, feat_n, hid, prods, part, x_sum, x_in, y_in, d_in, grad_t,
     back, slabs, pbuf, sbuf, rbuf, gwbuf, gwpair, gwsum, gwrow, gwmine, gwcol, plan_v, plan_s,
     l_sem, a_send, a_recv, f_send, f_recv, r_send, r_recv, g_send, g_recv,
@@ -333,6 +329,8 @@
     steps = {"f": first, "s": second, "e": finish, "g": spread, "d": drain}
     for step in SCHEDULE.split():
         steps[step[0]](int(step[1]))
+    act_copy = pltpu.make_async_copy(act, act_out, l_sem.at[8])
+    act_copy.start()
     for key in list(gathers):
         here(*key)
 
@@ -359,24 +357,22 @@
             back[b] = block
             out = jnp.dot(w, block, preferred_element_type=f32)
             span = pl.ds(pl.multiple_of(b * BLK, BLK), BLK)
-            slabs[:, :, span] = out.reshape(NROW, PER, BLK).astype(bf16)
+            slabs[:, :, :, span] = out.reshape(NROW // 2, 2, PER, BLK).astype(bf16)
             total = total + jnp.dot(block, feat_n[b], preferred_element_type=f32)
         return total
 
-    def start_pairs(h, items):
-        for dy, dz in items:
-            k = chips.index((dy, dz))
-            pairs[dy, dz, h] = start_remote(
-                pending,
-                half(slabs.at[at(dy, dz, other)], h),
-                pbuf.at[h, k],
-                p_send.at[h, k],
-                p_recv.at[h, k],
-                row=partner,
-            )
+    def start_pairs(h):
+        pairs[h] = start_remote(
+            pending,
+            slabs.at[:, other, :, pl.ds(h * HALF, HALF)],
+            pbuf.at[h],
+            p_send.at[h],
+            p_recv.at[h],
+            row=partner,
+        )
 
     gw_part = lax.fori_loop(0, BC // 32, panel_step, jnp.zeros((F, F), f32))
-    start_pairs(0, [(0, 2), (1, 2), (0, 1), (1, 1), (0, 3), (1, 3), (1, 0), (0, 0)])
+    start_pairs(0)
     gw_part = lax.fori_loop(BC // 32, BC // 16, panel_step, gw_part)
     gw_part = gw_part.T
     for r in range(NROW):
@@ -387,10 +383,11 @@
 
 
     def pair_sum(dy, dz, h):
-        pairs[dy, dz, h].wait_recv()
-        k = chips.index((dy, dz))
-        own = slabs[at(dy, dz, core), :, h * HALF : (h + 1) * HALF]
-        return own.astype(f32) + pbuf[h, k].astype(f32)
+        if h in pairs:
+            pairs.pop(h).wait_recv()
+        chip = ((yh + dy) % 2) * 4 + (z + dz) % 4
+        own = slabs[chip, core, :, h * HALF : (h + 1) * HALF]
+        return own.astype(f32) + pbuf[h, chip].astype(f32)
 
     def pass_sum(value, h, k, to):
         sbuf[h, k] = value.astype(bf16)
@@ -398,7 +395,7 @@
             pending, sbuf.at[h, k], rbuf.at[h, k], s_send.at[h, k], s_recv.at[h, k], row=to
         )
 
-    start_pairs(1, [(1, 2), (1, 1), (1, 3), (1, 0), (0, 2), (0, 1), (0, 3), (0, 0)])
+    start_pairs(1)
 
     gw_pair.wait_recv()
     gwsum[...] = gwbuf[core] + gwpair[...]
@@ -458,19 +455,27 @@
         sums[0, dz, 1].wait_recv()
         total = total + rbuf[1, chips.index((0, dz))].astype(f32)
     gf[:, HALF:] = total.astype(bf16)
+    outs = [act_copy, pltpu.make_async_copy(half(gf, 1), half(gf_out, 1), l_sem.at[9])]
+    outs[1].start()
 
     total = pair_sum(0, 0, 0)
     for dy, dz in ((0, 1), (0, 2), (0, 3), (1, 0)):
         sums[dy, dz, 0].wait_recv()
         total = total + rbuf[0, chips.index((dy, dz))].astype(f32)
     gf[:, :HALF] = total.astype(bf16)
+    outs.append(pltpu.make_async_copy(half(gf, 0), half(gf_out, 0), l_sem.at[10]))
+    outs[2].start()
 
     for k in range(1, NCOL):
         spreads[k - 1].wait_recv()
         gw_sum = gw_sum + gwcol[k]
     gw[...] = gw_sum
+    outs.append(pltpu.make_async_copy(gw, gw_out, l_sem.at[11]))
+    outs[3].start()
     for copy in pending:
         copy.wait_send()
+    for copy in outs:
+        copy.wait()
 
 
 def write_kernel(act, gw, gf, act_out, gw_out, gf_out, act_v, gw_v, gf_v, sem):
@@ -501,8 +506,9 @@
         layer_kernel,
         out_shape=shapes,
         in_specs=[any_spec()] * 7,
-        out_specs=(vmem_spec(), vmem_spec(), vmem_spec()),
+        out_specs=(any_spec(),) * 3,
         scratch_shapes=[
+            *(pltpu.VMEM(x.shape, x.dtype) for x in shapes),
             pltpu.VMEM((F, F), bf16),
             pltpu.VMEM((1, TILE_CAP), i32),
             pltpu.VMEM((1, TILE_CAP), i32),
@@ -520,7 +526,7 @@
             pltpu.VMEM((NSUB, NCOL - 1, WIDE * BLK, F), bf16),
             pltpu.VMEM((BR, F, BLK), bf16),
             pltpu.VMEM((BC, F, BLK), bf16),
-            pltpu.VMEM((NROW, PER, PANEL), bf16),
+            pltpu.VMEM((NROW // 2, 2, PER, PANEL), bf16),
             pltpu.VMEM((2, 8, PER, HALF), bf16),
             pltpu.VMEM((2, 7, PER, HALF), bf16),
             pltpu.VMEM((2, 7, PER, HALF), bf16),
@@ -532,9 +538,9 @@
             pltpu.VMEM((NCOL, PER, F), f32),
             pltpu.VMEM((16, TILE_CAP), i32),
             pltpu.SMEM((16, TILE_CAP), i32),
-            dma(8), dma(16), dma(16), dma(15), dma(15),
+            dma(12), dma(16), dma(16), dma(15), dma(15),
             dma(16, NSUB), dma(16, NSUB), dma(NCOL, NSUB), dma(NCOL, NSUB),
-            dma(2, 8), dma(2, 8), dma(2, 7), dma(2, 7), dma(8), dma(8),
+            dma(2), dma(2), dma(2, 7), dma(2, 7), dma(8), dma(8),
             dma(NCOL), dma(NCOL),
         ],
         compiler_params=pltpu.CompilerParams(

time: 70.4 us -> 69.9 us (level)
  Pallas kernels: 68.3 us -> 67.4 us
    pallas_call x1, Pallas kernels: 66.6 us -> 65.8 us  [on_device(): pl.pallas_call(layer_kernel, out_shape=shapes, in_specs=[any_spec()] * 7,...]
where the time goes in v6:
time: 69.9 us; the launch traced here: 68.7 us
  Pallas kernels  67.4 us (96%)
  between operations  1.29 us (2%)
    pallas_call x1, Pallas kernels, on_device(): pl.pallas_call(layer_kernel, out_shape=shapes, in_specs=[any_spec()] * 7,...  65.8 us
    pallas_call x1, Pallas kernels, on_device(): pl.pallas_call(write_kernel, out_shape=shapes, in_specs=[any_spec()] * 3,...  1.68 us

profile of v6, /device:TPU:0, one launch (start us, length us, event | category | flops | bytes accessed | tf_op | source)
XLA Modules:
  0.0 68.7 jit_solution(4883060317972371237)
XLA Ops:
  1.3 65.8 %graph_layer.1 = (bf16[512,128]{1,0:T(8,128)(2,1)}, f32[8,128]{1,0:T(8,128)}, bf16[8,8192]{1,0:T(8,128)(2,1)}) custom-call(bf16[8,8192]{1,0:T(8,128)(2,1)} %bitcast.4, bf16[128,128]{1,0:T(8,128)(2,1)} %weight_in.1, bf16[1,1,256,128,128]{4,3,2,1,0:T(8,128)(2,1)} %tiles.1, s32[1,256]{1,0:T(1,128)} %bitcast.5, s32[1,256]{1,0:T(1,128)} %bitcast.6, ...), custom_call_target="tpu_custom_call" | custom-call | flops 2147483648 | bytes 11534336 | tf_op jit(solution)/shard_map/graph_layer/pallas_call | solution.py:505
  67.0 1.7 %write_results.1 = (bf16[512,128]{1,0:T(8,128)(2,1)}, f32[8,128]{1,0:T(8,128)}, bf16[8,8192]{1,0:T(8,128)(2,1)}) custom-call(bf16[512,128]{1,0:T(8,128)(2,1)} %get-tuple-element.9.act, f32[8,128]{1,0:T(8,128)} %get-tuple-element.10.gw, bf16[8,8192]{1,0:T(8,128)(2,1)} %get-tuple-element.11.gf), custom_call_target="tpu_custom_call" | custom-call | tf_op jit(solution)/shard_map/write_results/pallas_call | solution.py:554

commit v7 on v6

--- a/solution.py
+++ b/solution.py
@@ -422,13 +422,6 @@
         k = chips.index((1, dz))
         sums[1, dz, 1] = pass_sum(pair_sum(1, dz, 1), 1, k, across)
 
-    for dz in (2, 1, 3):
-        k = chips.index((0, dz))
-        value = pair_sum(0, dz, 1)
-        sums[1, dz, 1].wait_recv()
-        value = value + rbuf[1, chips.index((1, dz))].astype(f32)
-        sums[0, dz, 1] = pass_sum(value, 1, k, at(0, dz, core))
-
     gw_sum = gwsum[me // 2]
     for k in range(7):
         shares[k].wait_recv()
@@ -441,6 +434,13 @@
                 pending, gwmine, gwcol.at[k], c_send.at[k], c_recv.at[k], col=cpeers[k - 1]
             )
         )
+
+    for dz in (2, 1, 3):
+        k = chips.index((0, dz))
+        value = pair_sum(0, dz, 1)
+        sums[1, dz, 1].wait_recv()
+        value = value + rbuf[1, chips.index((1, dz))].astype(f32)
+        sums[0, dz, 1] = pass_sum(value, 1, k, at(0, dz, core))
 
     value = pair_sum(1, 0, 0)
     for dz in (1, 2, 3):

time: 69.9 us -> 69.7 us (level)
  no operation moved by 1% of the time
where the time goes in v7:
time: 69.7 us; the launch traced here: 68.5 us
  Pallas kernels  67.2 us (96%)
  between operations  1.29 us (2%)
    pallas_call x1, Pallas kernels, on_device(): pl.pallas_call(layer_kernel, out_shape=shapes, in_specs=[any_spec()] * 7,...  65.5 us
    pallas_call x1, Pallas kernels, on_device(): pl.pallas_call(write_kernel, out_shape=shapes, in_specs=[any_spec()] * 3,...  1.68 us

profile of v7, /device:TPU:0, one launch (start us, length us, event | category | flops | bytes accessed | tf_op | source)
XLA Modules:
  0.0 68.5 jit_solution(913685271189589740)
XLA Ops:
  1.3 65.5 %graph_layer.1 = (bf16[512,128]{1,0:T(8,128)(2,1)}, f32[8,128]{1,0:T(8,128)}, bf16[8,8192]{1,0:T(8,128)(2,1)}) custom-call(bf16[8,8192]{1,0:T(8,128)(2,1)} %bitcast.4, bf16[128,128]{1,0:T(8,128)(2,1)} %weight_in.1, bf16[1,1,256,128,128]{4,3,2,1,0:T(8,128)(2,1)} %tiles.1, s32[1,256]{1,0:T(1,128)} %bitcast.5, s32[1,256]{1,0:T(1,128)} %bitcast.6, ...), custom_call_target="tpu_custom_call" | custom-call | flops 2147483648 | bytes 11534336 | tf_op jit(solution)/shard_map/graph_layer/pallas_call | solution.py:505
  66.8 1.7 %write_results.1 = (bf16[512,128]{1,0:T(8,128)(2,1)}, f32[8,128]{1,0:T(8,128)}, bf16[8,8192]{1,0:T(8,128)(2,1)}) custom-call(bf16[512,128]{1,0:T(8,128)(2,1)} %get-tuple-element.9.act, f32[8,128]{1,0:T(8,128)} %get-tuple-element.10.gw, bf16[8,8192]{1,0:T(8,128)(2,1)} %get-tuple-element.11.gf), custom_call_target="tpu_custom_call" | custom-call | tf_op jit(solution)/shard_map/write_results/pallas_call | solution.py:554

commit v8 on v7

--- a/solution.py
+++ b/solution.py
@@ -135,12 +135,12 @@
             pending, src, piece, a_send.at[index], a_recv.at[index], row=at(ty, tz, core)
         )
 
+    for tz in (2, 1, 3):
+        send(0, 0, 0, 0, tz)
     send(0, 0, 1, 1, 0)
     for tz in (2, 1, 3):
-        send(0, 0, 0, 0, tz)
+        send(0, 0, 1, 0, tz)
     send(0, 0, 0, 1, 0)
-    for tz in (2, 1, 3):
-        send(0, 0, 1, 0, tz)
     own_hand = start_remote(
         pending, feat_in, feat.at[me], f_send.at[0], f_recv.at[0], row=partner
     )

time: 69.7 us -> 69.6 us (level)
  no operation moved by 1% of the time
where the time goes in v8:
time: 69.6 us; the launch traced here: 68.7 us
  Pallas kernels  67.5 us (97%)
  between operations  1.29 us (2%)
    pallas_call x1, Pallas kernels, on_device(): pl.pallas_call(layer_kernel, out_shape=shapes, in_specs=[any_spec()] * 7,...  65.8 us
    pallas_call x1, Pallas kernels, on_device(): pl.pallas_call(write_kernel, out_shape=shapes, in_specs=[any_spec()] * 3,...  1.68 us

profile of v8, /device:TPU:0, one launch (start us, length us, event | category | flops | bytes accessed | tf_op | source)
XLA Modules:
  0.0 68.7 jit_solution(17445188316086998055)
XLA Ops:
  1.3 65.8 %graph_layer.1 = (bf16[512,128]{1,0:T(8,128)(2,1)}, f32[8,128]{1,0:T(8,128)}, bf16[8,8192]{1,0:T(8,128)(2,1)}) custom-call(bf16[8,8192]{1,0:T(8,128)(2,1)} %bitcast.4, bf16[128,128]{1,0:T(8,128)(2,1)} %weight_in.1, bf16[1,1,256,128,128]{4,3,2,1,0:T(8,128)(2,1)} %tiles.1, s32[1,256]{1,0:T(1,128)} %bitcast.5, s32[1,256]{1,0:T(1,128)} %bitcast.6, ...), custom_call_target="tpu_custom_call" | custom-call | flops 2147483648 | bytes 11534336 | tf_op jit(solution)/shard_map/graph_layer/pallas_call | solution.py:505
  67.1 1.7 %write_results.1 = (bf16[512,128]{1,0:T(8,128)(2,1)}, f32[8,128]{1,0:T(8,128)}, bf16[8,8192]{1,0:T(8,128)(2,1)}) custom-call(bf16[512,128]{1,0:T(8,128)(2,1)} %get-tuple-element.9.act, f32[8,128]{1,0:T(8,128)} %get-tuple-element.10.gw, bf16[8,8192]{1,0:T(8,128)(2,1)} %get-tuple-element.11.gf), custom_call_target="tpu_custom_call" | custom-call | tf_op jit(solution)/shard_map/write_results/pallas_call | solution.py:554
